TPU v7x, 32 devices: a whole 2x2x4 slice. The times are simulated.
32 devices in a mesh: hid: 4 (over x, core), ep: 8 (over z, y).
Axes of the slice: x: 2, y: 2, z: 4, core: 2. Of those that a mesh axis runs over, the one named last changes fastest.
Arguments:
- gate_proj: bfloat16 [2, 7168, 2048], P(None, 'hid', 'ep'), may hold values from -6 to 6
- up_proj: bfloat16 [2, 7168, 2048], P(None, 'hid', 'ep'), may hold values from -6 to 6
- down_proj: bfloat16 [2, 2048, 7168], P(None, 'ep', 'hid'), may hold values from -6 to 6
- rotation: bfloat16 [7168, 7168], P('hid'), may hold values from -0.0625 to 0.0625
- placement: int32 [2, 8], replicated, may hold values from 0 to 7, each once within a row
- row_count: int32 [2, 8], replicated, may hold values from 64 to 512, as said below
Outputs:
- served: bfloat16 [8, 1024, 3, 7168], P('ep', 'hid')
Inputs may be any that keep to these rules, and one draw needn't show every extreme that they name: `row_count`: every count is a multiple of 64, each expert's counts sum to 2048, and one owner holds 512 rows of every expert.
All inputs are finite; a program needn't handle non-finite values.
Results may differ from a plain program's by a relative error of at most 0.017.
Values may be sent and summed in bfloat16 or wider, within the bound.
No kernel may reach another device: no remote copies, remote signals or barrier semaphores. Data moves between devices by JAX's collectives and lax.ppermute only.
A program may use at most 192 MiB of HBM per device.

v0:
```python
import jax
import jax.numpy as jnp
from jax import lax
from jax.sharding import PartitionSpec as P


def count_below(bound, residue, shard_total):
    return (bound + shard_total - 1 - residue) // shard_total


def routing(placement, row_count, block_rows):
    owner_total = placement.shape[1]
    blocks = row_count // block_rows
    onehot = (
        placement[:, :, None] == jnp.arange(owner_total, dtype=jnp.int32)[None, None, :]
    ).astype(jnp.int32)
    ordered = jnp.sum(onehot * blocks[:, None, :], axis=2)
    ordered_start = jnp.cumsum(ordered, axis=1) - ordered
    first_block = jnp.sum(onehot * ordered_start[:, :, None], axis=1)
    return (blocks, first_block)


def assemble(received, received_slot, slot_blocks, experts):
    flat_slot = received_slot.reshape(-1)
    matches = flat_slot[None, :] == jnp.arange(slot_blocks, dtype=jnp.int32)[:, None]
    present = jnp.any(matches, axis=1)
    picked = jnp.argmax(matches, axis=1)
    source_ids = picked // experts
    expert_ids = picked % experts
    chosen = received[source_ids, :, expert_ids]
    chosen = jnp.where(present[:, None, None, None], chosen, jnp.zeros((), jnp.bfloat16))
    return chosen.reshape(1, slot_blocks * chosen.shape[1], chosen.shape[2], chosen.shape[3])


def on_device(gate_proj, up_proj, down_proj, rotation, placement, row_count):
    shard_total = lax.axis_size("hid")
    owner_total = lax.axis_size("ep")
    experts, width_part, local_rows = gate_proj.shape
    full_width = rotation.shape[1]
    block_rows = local_rows // shard_total
    stacked = jnp.stack(
        [
            jnp.transpose(gate_proj, (2, 0, 1)),
            jnp.transpose(up_proj, (2, 0, 1)),
            jnp.transpose(down_proj, (1, 0, 2)),
        ],
        axis=2,
    )
    stacked = stacked.reshape(local_rows, experts * 3, width_part)
    summed = lax.psum_scatter(
        jnp.einsum("fck,kh->fch", stacked, rotation, preferred_element_type=jnp.float32).astype(
            jnp.bfloat16
        ),
        "hid",
        scatter_dimension=0,
        tiled=True,
    )
    rotated = summed.reshape(block_rows, experts, 3, full_width)
    shard_here = lax.axis_index("hid")
    owner_here = lax.axis_index("ep")
    block_here = owner_here * shard_total + shard_here
    blocks, first_block = routing(placement, row_count, block_rows)
    inside = ((first_block <= block_here) & (block_here < first_block + blocks)).astype(jnp.int32)
    owner_ids = jnp.arange(owner_total, dtype=jnp.int32)
    target_owner = jnp.sum(inside * owner_ids[None, :], axis=1)
    at_shard = count_below(first_block + blocks, shard_here, shard_total) - count_below(
        first_block, shard_here, shard_total
    )
    offset = jnp.cumsum(at_shard, axis=0) - at_shard
    slot_index = jnp.sum(
        inside * (offset - count_below(first_block, shard_here, shard_total)), axis=1
    )
    slot_index = slot_index + count_below(block_here, shard_here, shard_total)
    slot_blocks = 2 * experts
    all_blocks, all_owner, all_slot = (
        lax.all_gather(rotated[None], "ep", axis=0, tiled=True),
        lax.all_gather(target_owner[None], "ep", axis=0, tiled=True),
        lax.all_gather(slot_index[None], "ep", axis=0, tiled=True),
    )
    received_slot = jnp.where(all_owner == owner_here, all_slot, -1)
    return assemble(all_blocks, received_slot, slot_blocks, experts)


def solution(mesh):
    in_specs = (
        P(None, "hid", "ep"),
        P(None, "hid", "ep"),
        P(None, "ep", "hid"),
        P("hid", None),
        P(),
        P(),
    )
    out_specs = P("ep", "hid", None, None)
    return jax.shard_map(
        on_device, mesh=mesh, in_specs=in_specs, out_specs=out_specs, check_vma=False
    )
```

profile of v0, /device:TPU:0, one launch (start us, length us, event | category | flops | bytes accessed | tf_op | source)
XLA Modules:
  0.0 1131.5 jit_solution(10768781958453358871)
XLA Ops:
  6.5 2.8 copy.22
  9.3 3.8 copy.21
  13.2 3.0 pad_maximum_fusion.1
  16.2 0.4 copy.23
  16.5 46.1 %fusion.2 = bf16[256,6,7168]{2,0,1:T(8,128)(2,1)} fusion(bf16[256,6,1792]{2,0,1:T(8,128)(2,1)S(1)} %bitcast.22, bf16[1792,7168]{1,0:T(8,128)(2,1)} %param.9), kind=kOutput, calls=%fused_computation.4 | convolution fusion | flops 39471022080 | bytes 53215232 | tf_op jit(solution)/shard_map/fck,kh->fch/dot_general | solution.py:51
  62.7 162.7 %reduce-scatter.2.cloned.1.call-done = bf16[64,6,7168]{2,0,1:T(8,128)(2,1)} async-done(((bf16[256,6,7168]{2,0,1:T(8,128)(2,1)}), bf16[64,6,7168]{2,0,1:T(8,128)(2,1)}) %reduce-scatter.2.cloned.1.call-update) | async-done | bytes 5505040 | tf_op jit(solution)/shard_map/reduce_scatter | solution.py:50
  225.5 0.2 select_reduce_fusion.1
  225.7 0.2 reduce_window_sum.22
  225.9 0.6 dynamic-slice
  227.1 0.1 select_reduce_fusion
  227.3 0.2 select_reduce_fusion.3
  227.4 0.1 add_dynamic-update-slice_fusion
  227.5 0.2 dynamic-update-slice
  227.7 11.5 %all-reduce.2 = (s32[16]{0:T(128)S(1)}, s32[16]{0:T(128)S(1)}) all-reduce(s32[16]{0:T(128)S(1)} %add_dynamic-update-slice_fusion, s32[16]{0:T(128)S(1)} %dynamic-update-slice), channel_id=3, replica_groups=mesh['hid'=4,'ep'=8] {'ep'}, use_global_device_ids=true, to_apply=%add.1 | all-reduce | flops 32 | bytes 256
  239.2 0.1 fusion.5
  239.4 0.1 broadcast_in_dim.40
  239.5 0.6 iota_reduce_fusion
  240.2 821.2 %all-gather.4.cloned.1.call-done = bf16[8,64,2,3,7168]{4,1,3,2,0:T(8,128)(2,1)} async-done(((bf16[1,64,2,3,7168]{4,1,3,2,0:T(8,128)(2,1)}), bf16[8,64,2,3,7168]{4,1,3,2,0:T(8,128)(2,1)}) %all-gather.4.cloned.1.call-update) | async-done | bytes 44040208 | tf_op jit(solution)/shard_map/all_gather | solution.py:76
  1061.4 29.2 %fusion.12 = (bf16[8,64,2,3,3584]{4,1,3,2,0:T(8,128)(2,1)}, bf16[8,64,2,3,3584]{4,1,3,2,0:T(8,128)(2,1)}) fusion(bf16[8,64,2,3,7168]{4,1,3,2,0:T(8,128)(2,1)} %all-gather.4.cloned.1.call-done), kind=kLoop, calls=%fused_computation.44 | loop fusion | bytes 88080384 | tf_op jit(solution)/shard_map/gather | solution.py:30
  1090.6 10.6 gather_fusion.1
  1101.2 10.5 gather_fusion
  1111.8 5.8 pad_maximum_fusion
  1117.6 1.8 copy.24
  1119.4 5.3 bitcast_select_fusion
  (19 shorter events, 0.3 us)
Async XLA Ops:
  6.5 218.9 %reduce-scatter.2.cloned.1.call-start = ((), (), s32[]{:S(2)}) async-start(), calls=%async_computation.1 | async-start | bytes 27525120 | tf_op jit(solution)/shard_map/reduce_scatter | solution.py:50
  62.6 162.8 %copy-start = (s32[2,8]{1,0:T(2,128)S(1)}, s32[2,8]{1,0:T(2,128)}, u32[]{:S(2)}) copy-start(s32[2,8]{1,0:T(2,128)} %param.11) | copy-start | bytes 196
  62.6 162.9 %copy-start.1 = (s32[2,8]{1,0:T(2,128)S(1)}, s32[2,8]{1,0:T(2,128)}, u32[]{:S(2)}) copy-start(s32[2,8]{1,0:T(2,128)} %param.10) | copy-start | bytes 196
  62.6 163.3 %copy-start.2 = (u32[32]{0:T(128)S(1)}, u32[32]{0:T(128)}, u32[]{:S(2)}) copy-start(u32[32]{0:T(128)} %constant.137) | copy-start | bytes 388
  62.6 998.8 %all-gather.4.cloned.1.call-start = ((), (), s32[]{:S(2)}) async-start(), calls=%async_computation.2 | async-start | bytes 49545216 | tf_op jit(solution)/shard_map/all_gather | solution.py:76
Sparse Core Ops, SparseCore 0:
  62.7 162.5 reduce-scatter.1
  227.0 834.3 all-gather.3
where the time goes:
time: 1130 us
  waiting for transfers between devices  984 us (87%)
  local copies, waits for them, and re-layouts  60.1 us (5%)
  matrix products  46.1 us (4%)
  other arithmetic  15.7 us (1%)
  between operations  14.2 us (1%)
  blocking collectives  11.5 us (1%)
    all_gather x1, waiting for transfers between devices, on_device(): lax.all_gather(rotated[None], 'ep', axis=0, tiled=True)  821 us
    reduce_scatter x1, waiting for transfers between devices, on_device(): lax.psum_scatter(jnp.einsum('fck,kh->fch', stacked, rotation, preferred_e...  163 us
    gather x3, local copies, waits for them, and re-layouts, assemble(): chosen = received[source_ids, :, expert_ids]  50.4 us
    dot_general x1, matrix products, on_device(): jnp.einsum('fck,kh->fch', stacked, rotation, preferred_element_type=jnp.f...  46.1 us
  transfers between devices with their start and end apart: 2, of which 2 were waited for; matrix products, arithmetic and copies ran while one was open for 0% of the time, Pallas kernels for 0%

commit v1 on v0

--- a/solution.py
+++ b/solution.py
@@ -1,7 +1,564 @@
+import functools
+
 import jax
 import jax.numpy as jnp
 from jax import lax
+from jax.experimental import pallas as pl
+from jax.experimental.pallas import tpu as pltpu
 from jax.sharding import PartitionSpec as P
+
+CHUNK_TILES = (1, 1, 2, 2, 2, 2, 2, 1, 1)
+MATMUL_VMEM = 16 * 2**20
+MOVE_VMEM = 8 * 2**20
+COST = pl.CostEstimate(flops=20000000000, bytes_accessed=2**10, transcendentals=0)
+ORDER = (
+    'S0',
+    'S1',
+    'S2',
+    'K0',
+    'K1',
+    'K2',
+    'A0',
+    'S3',
+    'A1',
+    'I0',
+    'K3',
+    'I1',
+    'M0',
+    'A2',
+    'S4',
+    'M1',
+    'I2',
+    'K4',
+    'O0',
+    'A3',
+    'M2',
+    'I3',
+    'O1',
+    'A4',
+    'P0',
+    'I4',
+    'M3',
+    'P1',
+    'L0',
+    'S5',
+    'O2',
+    'L1',
+    'K5',
+    'S6',
+    'M4',
+    'K6',
+    'A5',
+    'O3',
+    'P2',
+    'I5',
+    'A6',
+    'L2',
+    'S7',
+    'M5',
+    'I6',
+    'O4',
+    'K7',
+    'P3',
+    'A7',
+    'M6',
+    'L3',
+    'S8',
+    'I7',
+    'O5',
+    'K8',
+    'P4',
+    'M7',
+    'A8',
+    'L4',
+    'O6',
+    'I8',
+    'P5',
+    'M8',
+    'O7',
+    'L5',
+    'O8',
+    'P6',
+    'P7',
+    'L6',
+    'L7',
+    'P8',
+    'L8',
+)
+MARK = jax.ShapeDtypeStruct((8, 128), jnp.float32)
+KINDS = 3
+SLOT_TOTAL = 4
+ROWS_Z = 4
+LINK_CAP = 8
+AT_MID, AT_OUT, AT_PARTNER, AT_OWN, TABLE = 0, 8, 16, 20, 32
+KEEP, SIDE, FAR_KEEP, FAR_SIDE, MID, OUT, CODES = 0, 2, 4, 6, 8, 16, 24
+NEAR_CODES, FAR_CODES, MID_CODES, OUT_CODES = (0, 4), (4, 8), (8, 16), (16, 24)
+
+
+def route_kernel(here_ref, placement_ref, row_count_ref, table_ref, *, owners, hid_total, block_rows):
+    hid, ep = here_ref[0], here_ref[1]
+    z, y = ep // 2, ep % 2
+    experts = placement_ref.shape[0]
+    pieces = [(e, s) for e in range(experts) for s in range(owners)]
+    owner = {}
+    for e in range(experts):
+        start = jnp.int32(0)
+        found = [jnp.int32(0)] * owners
+        for j in range(owners):
+            o = placement_ref[e, j]
+            stop = start + row_count_ref[e, o] // block_rows
+            for s in range(owners):
+                q = s * hid_total + hid
+                found[s] = jnp.where((start <= q) & (q < stop), o, found[s])
+            start = stop
+        for s in range(owners):
+            owner[e, s] = found[s]
+    upper = z >= 2
+    mid_row = (z == 1) | (z == 2)
+
+    def half(row):
+        return row >= 2
+
+    zero = jnp.int32(0)
+    mid_in, mid_out, out_in, out_out = zero, zero, zero, zero
+    for i in range(TABLE):
+        table_ref[i] = jnp.int32(-1)
+    mine, partner = zero, zero
+    for e, s in pieces:
+        row, side = s // 2, s % 2
+        o = owner[e, s]
+        drow = o // 2
+        goes_up, goes_down = drow >= 2, drow < 2
+        crosses = goes_up if row < 2 else goes_down
+        from_here_half = jnp.logical_not(upper) if row < 2 else upper
+        leaves_mid = crosses & from_here_half
+        enters_mid = crosses & jnp.logical_not(from_here_half)
+        to_top = (drow == ROWS_Z - 1) if row < ROWS_Z - 1 else jnp.bool_(False)
+        to_bottom = (drow == 0) if row > 0 else jnp.bool_(False)
+        on_outer = jnp.where(upper, to_top, to_bottom)
+        near_far = z == row
+        outer_row = jnp.where(upper, ROWS_Z - 1, 0)
+        from_outer = mid_row & (outer_row == row)
+        code = jnp.where(
+            near_far,
+            jnp.where(y == side, KEEP + e, SIDE + e),
+            jnp.where(
+                from_outer,
+                jnp.where(y == side, FAR_KEEP + e, FAR_SIDE + e),
+                jnp.where(mid_row, MID + mid_in, OUT + out_in),
+            ),
+        )
+
+        @pl.when(leaves_mid & mid_row)
+        def _(mid_out=mid_out, code=code):
+            table_ref[AT_MID + mid_out] = code
+
+        @pl.when(on_outer & mid_row)
+        def _(out_in=out_in, code=code):
+            table_ref[AT_OUT + out_in] = code
+
+        is_mine = o == ep
+        is_partner = (drow == z) & (o != ep)
+
+        @pl.when(is_mine)
+        def _(mine=mine, code=code):
+            table_ref[AT_OWN + mine] = code
+
+        @pl.when(is_partner)
+        def _(partner=partner, code=code):
+            table_ref[AT_PARTNER + partner] = code
+
+        mid_out = mid_out + leaves_mid.astype(jnp.int32)
+        mid_in = mid_in + enters_mid.astype(jnp.int32)
+        out_in = out_in + on_outer.astype(jnp.int32)
+        mine = mine + is_mine.astype(jnp.int32)
+        partner = partner + is_partner.astype(jnp.int32)
+
+
+def route(here, placement, row_count, hid_total, block_rows):
+    smem = pl.BlockSpec(memory_space=pltpu.SMEM)
+    return pl.pallas_call(
+        functools.partial(
+            route_kernel,
+            owners=placement.shape[1],
+            hid_total=hid_total,
+            block_rows=block_rows,
+        ),
+        out_shape=jax.ShapeDtypeStruct((TABLE,), jnp.int32),
+        in_specs=[smem] * 3,
+        out_specs=smem,
+        compiler_params=pltpu.CompilerParams(vmem_limit_bytes=MOVE_VMEM),
+        name="route",
+    )(here, placement, row_count)
+
+
+ANYWHERE = pl.BlockSpec(memory_space=pl.ANY)
+ON_SMEM = pl.BlockSpec(memory_space=pltpu.SMEM)
+ON_VMEM = pl.BlockSpec(memory_space=pltpu.VMEM)
+TILE = 512
+
+
+def gather_rows_kernel(gate_ref, up_ref, down_ref, out_ref):
+    rows = out_ref.shape[4]
+    for kind, ref in enumerate((gate_ref, up_ref, down_ref)):
+        block = ref[0] if kind == 2 else ref[0].T
+        for x in range(2):
+            for core in range(2):
+                first = (2 * x + core) * rows
+                out_ref[core, x, 0, kind] = block[first : first + rows]
+
+
+def gather_rows(gate_proj, up_proj, down_proj):
+    experts, depth, local_rows = gate_proj.shape
+    block_rows = local_rows // 4
+    across = pl.BlockSpec((1, depth, local_rows), lambda e: (e, 0, 0))
+    along = pl.BlockSpec((1, local_rows, depth), lambda e: (e, 0, 0))
+    rows = pl.pallas_call(
+        gather_rows_kernel,
+        out_shape=jax.ShapeDtypeStruct((2, 2, experts, KINDS, block_rows, depth), jnp.bfloat16),
+        grid=(experts,),
+        in_specs=[across, across, along],
+        out_specs=pl.BlockSpec(
+            (2, 2, 1, KINDS, block_rows, depth), lambda e: (0, 0, e, 0, 0, 0)
+        ),
+        compiler_params=pltpu.CompilerParams(vmem_limit_bytes=32 * 2**20),
+        name="gather_rows",
+    )(gate_proj, up_proj, down_proj)
+    return rows.reshape(2, 2 * experts * KINDS * block_rows, depth)
+
+
+def product(lhs_ref, top_ref, bottom_ref):
+    depth = top_ref.shape[0]
+    return jnp.dot(
+        lhs_ref[0, :, :depth], top_ref[...], preferred_element_type=jnp.float32
+    ) + jnp.dot(lhs_ref[0, :, depth:], bottom_ref[...], preferred_element_type=jnp.float32)
+
+
+def send_kernel(here_ref, lhs_ref, top_ref, bottom_ref, after_ref, out_ref, mark_ref):
+    out_ref[...] = product(lhs_ref, top_ref, bottom_ref).astype(jnp.bfloat16)
+
+
+def keep_kernel(
+    here_ref, lhs_ref, top_ref, bottom_ref, recv_ref, after_ref, away_ref, home_ref, mark_ref
+):
+    rows = away_ref.shape[0]
+    total = product(lhs_ref, top_ref, bottom_ref) + recv_ref[...].astype(jnp.float32)
+    total = total.astype(jnp.bfloat16)
+    x = here_ref[0] // 2
+
+    @pl.when(x == 0)
+    def _():
+        home_ref[...] = total[:rows]
+        away_ref[...] = total[rows:]
+
+    @pl.when(x == 1)
+    def _():
+        home_ref[...] = total[rows:]
+        away_ref[...] = total[:rows]
+
+
+def matmul_specs(lhs, column, send):
+    _, rows, depth = lhs.shape
+
+    def lhs_map(tile, here):
+        core = here[0] % 2
+        return (1 - core if send else core, 0, 0)
+
+    def rot_map(part, tile, here):
+        return (part, column // TILE + tile)
+
+    return [
+        pl.BlockSpec((1, rows, depth), lhs_map, pipeline_mode=pl.Buffered(1)),
+        pl.BlockSpec((depth // 2, TILE), functools.partial(rot_map, 0)),
+        pl.BlockSpec((depth // 2, TILE), functools.partial(rot_map, 1)),
+    ]
+
+
+def matmul_send(here, lhs, rotation, column, width, after, cost):
+    _, rows, _ = lhs.shape
+    return pl.pallas_call(
+        send_kernel,
+        out_shape=(jax.ShapeDtypeStruct((rows, width), jnp.bfloat16), MARK),
+        grid_spec=pltpu.PrefetchScalarGridSpec(
+            num_scalar_prefetch=1,
+            grid=(width // TILE,),
+            in_specs=matmul_specs(lhs, column, True) + [ANYWHERE],
+            out_specs=(pl.BlockSpec((rows, TILE), lambda t, here: (0, t)), ANYWHERE),
+        ),
+        compiler_params=pltpu.CompilerParams(vmem_limit_bytes=MATMUL_VMEM),
+        cost_estimate=cost,
+        name="matmul_send",
+    )(here, lhs, rotation, rotation, after)
+
+
+def matmul_keep(here, lhs, rotation, recv, column, width, after, cost):
+    _, rows, _ = lhs.shape
+    out = jax.ShapeDtypeStruct((rows // 2, width), jnp.bfloat16)
+    out_spec = pl.BlockSpec((rows // 2, TILE), lambda t, here: (0, t))
+    recv_spec = pl.BlockSpec((rows, TILE), lambda t, here: (0, t))
+    return pl.pallas_call(
+        keep_kernel,
+        out_shape=(out, out, MARK),
+        grid_spec=pltpu.PrefetchScalarGridSpec(
+            num_scalar_prefetch=1,
+            grid=(width // TILE,),
+            in_specs=matmul_specs(lhs, column, False) + [recv_spec, ANYWHERE],
+            out_specs=(out_spec, out_spec, ANYWHERE),
+        ),
+        compiler_params=pltpu.CompilerParams(vmem_limit_bytes=MATMUL_VMEM),
+        cost_estimate=cost,
+        name="matmul_keep",
+    )(here, lhs, rotation, rotation, recv, after)
+
+
+def add_kernel(here_ref, home_ref, recv_ref, after_ref, side_ref, keep_ref, mark_ref):
+    width = side_ref.shape[1]
+    y = here_ref[1] % 2
+    for half, ref in ((1 - y, side_ref), (y, keep_ref)):
+        part = pl.ds(pl.multiple_of(half * width, 128), width)
+        total = home_ref[:, part].astype(jnp.float32) + recv_ref[:, part].astype(jnp.float32)
+        ref[...] = total.astype(jnp.bfloat16)
+
+
+def add(here, home, recv, after, cost):
+    rows, width = home.shape
+    tile = 128
+    out = jax.ShapeDtypeStruct((rows, width // 2), jnp.bfloat16)
+    in_spec = pl.BlockSpec((tile, width), lambda i, here: (i, 0))
+    out_spec = pl.BlockSpec((tile, width // 2), lambda i, here: (i, 0))
+    return pl.pallas_call(
+        add_kernel,
+        out_shape=(out, out, MARK),
+        grid_spec=pltpu.PrefetchScalarGridSpec(
+            num_scalar_prefetch=1,
+            grid=(rows // tile,),
+            in_specs=[in_spec, in_spec, ANYWHERE],
+            out_specs=(out_spec, out_spec, ANYWHERE),
+        ),
+        compiler_params=pltpu.CompilerParams(vmem_limit_bytes=MOVE_VMEM),
+        cost_estimate=cost,
+        name="add",
+    )(here, home, recv, after)
+
+
+def start_pick(code, bases, sources, target, sem):
+    for source, (low, high) in zip(sources, bases):
+
+        @pl.when((code >= low) & (code < high))
+        def _(source=source, low=low):
+            pltpu.make_async_copy(source.at[code - low], target, sem).start()
+
+
+def pick_kernel(table_ref, *refs, first, bases):
+    sources, out_ref, sems = refs[: len(bases)], refs[-3], refs[-1]
+    total = out_ref.shape[0]
+    for i in range(total):
+        start_pick(table_ref[first + i], bases, sources, out_ref.at[i], sems.at[i])
+    for i in range(total):
+
+        @pl.when(table_ref[first + i] >= 0)
+        def _(i=i):
+            pltpu.make_async_copy(sources[0].at[0], out_ref.at[i], sems.at[i]).wait()
+
+
+def pick(table, sources, bases, first, total, after, cost):
+    piece = sources[0].shape[1:]
+    return pl.pallas_call(
+        functools.partial(pick_kernel, first=first, bases=bases),
+        out_shape=(jax.ShapeDtypeStruct((total,) + piece, jnp.bfloat16), MARK),
+        in_specs=[ON_SMEM] + [ANYWHERE] * (len(sources) + 1),
+        out_specs=(ON_VMEM, ANYWHERE),
+        scratch_shapes=[pltpu.SemaphoreType.DMA((total,))],
+        cost_estimate=cost,
+        compiler_params=pltpu.CompilerParams(vmem_limit_bytes=MOVE_VMEM),
+        name="pick",
+    )(table, *sources, after)
+
+
+def pack_kernel(keep_ref, side_ref, after_ref, out_ref, mark_ref, sems):
+    experts = keep_ref.shape[0]
+    copies = [
+        pltpu.make_async_copy(ref, out_ref.at[pl.ds(n * experts, experts)], sems.at[n])
+        for n, ref in enumerate((keep_ref, side_ref))
+    ]
+    for copy in copies:
+        copy.start()
+    for copy in copies:
+        copy.wait()
+
+
+def pack(keep, side, after, cost):
+    experts = keep.shape[0]
+    return pl.pallas_call(
+        pack_kernel,
+        out_shape=(jax.ShapeDtypeStruct((2 * experts,) + keep.shape[1:], jnp.bfloat16), MARK),
+        in_specs=[ANYWHERE] * 3,
+        out_specs=(ON_VMEM, ANYWHERE),
+        scratch_shapes=[pltpu.SemaphoreType.DMA((2,))],
+        compiler_params=pltpu.CompilerParams(vmem_limit_bytes=MOVE_VMEM),
+        cost_estimate=cost,
+        name="pack",
+    )(keep, side, after)
+
+
+def place_kernel(here_ref, table_ref, *refs, bases, column):
+    sources, partner_ref = refs[: len(bases)], refs[len(bases)]
+    out_ref, mark_ref, held_ref, in_sems, out_sems = refs[-5:]
+    _, _, _, rows, width = held_ref.shape
+    y = here_ref[1] % 2
+
+    def target(slot, half):
+        at = pl.multiple_of(column + half * width, 128)
+        return out_ref.at[:, pl.ds(slot * rows, rows), pl.ds(at, width)]
+
+    for slot in range(SLOT_TOTAL):
+        code = table_ref[AT_OWN + slot]
+        start_pick(code, bases, sources, held_ref.at[slot, 0], in_sems.at[slot, 0])
+
+        @pl.when(code >= 0)
+        def _(slot=slot):
+            pltpu.make_async_copy(
+                partner_ref.at[slot], held_ref.at[slot, 1], in_sems.at[slot, 1]
+            ).start()
+
+        @pl.when(code < 0)
+        def _(slot=slot):
+            held_ref[slot] = jnp.zeros(held_ref.shape[1:], held_ref.dtype)
+
+    for slot in range(SLOT_TOTAL):
+
+        @pl.when(table_ref[AT_OWN + slot] >= 0)
+        def _(slot=slot):
+            for part in range(2):
+                pltpu.make_async_copy(
+                    partner_ref.at[slot], held_ref.at[slot, part], in_sems.at[slot, part]
+                ).wait()
+
+        pltpu.make_async_copy(held_ref.at[slot, 0], target(slot, y), out_sems.at[slot, 0]).start()
+        pltpu.make_async_copy(
+            held_ref.at[slot, 1], target(slot, 1 - y), out_sems.at[slot, 1]
+        ).start()
+    for slot in range(SLOT_TOTAL):
+        pltpu.make_async_copy(held_ref.at[slot, 0], target(slot, y), out_sems.at[slot, 0]).wait()
+        pltpu.make_async_copy(
+            held_ref.at[slot, 1], target(slot, 1 - y), out_sems.at[slot, 1]
+        ).wait()
+
+
+def place(here, table, sources, bases, partner, column, full_width, previous, after, cost):
+    piece = partner.shape[1:]
+    operands = [here, table, *sources, partner, after]
+    in_specs = [ON_SMEM, ON_SMEM] + [ANYWHERE] * (len(sources) + 2)
+    aliases = {}
+    if previous is not None:
+        aliases = {len(operands): 0}
+        operands.append(previous)
+        in_specs.append(ANYWHERE)
+    return pl.pallas_call(
+        functools.partial(place_kernel, bases=bases, column=column),
+        out_shape=(
+            jax.ShapeDtypeStruct((KINDS, SLOT_TOTAL * piece[1], full_width), jnp.bfloat16),
+            MARK,
+        ),
+        in_specs=in_specs,
+        out_specs=(ANYWHERE, ANYWHERE),
+        scratch_shapes=[
+            pltpu.VMEM((SLOT_TOTAL, 2) + piece, jnp.bfloat16),
+            pltpu.SemaphoreType.DMA((SLOT_TOTAL, 2)),
+            pltpu.SemaphoreType.DMA((SLOT_TOTAL, 2)),
+        ],
+        input_output_aliases=aliases,
+        cost_estimate=cost,
+        compiler_params=pltpu.CompilerParams(vmem_limit_bytes=MOVE_VMEM),
+        name="place",
+    )(*operands)
+
+
+def pipelined(gate_proj, up_proj, down_proj, rotation, placement, row_count):
+    hid_total = lax.axis_size("hid")
+    experts, depth, local_rows = gate_proj.shape
+    full_width = rotation.shape[1]
+    block_rows = local_rows // hid_total
+    here = jnp.stack([lax.axis_index("hid"), lax.axis_index("ep")]).astype(jnp.int32)
+    table = route(here, placement, row_count, hid_total, block_rows)
+
+    lhs = gather_rows(gate_proj, up_proj, down_proj)
+
+    cores = [(h, h ^ 1) for h in range(4)]
+    along_x = [(h, h ^ 2) for h in range(4)]
+    along_y = [(s, s ^ 1) for s in range(8)]
+    inward = [(0, 2), (1, 3), (6, 4), (7, 5)]
+    middle = [(2, 4), (3, 5), (4, 2), (5, 3)]
+    outward = [(4, 6), (5, 7), (2, 0), (3, 1)]
+    widths = [tiles * TILE for tiles in CHUNK_TILES]
+    columns = [sum(widths[:i]) for i in range(len(widths))]
+    chunks = len(widths)
+
+    core_recv, x_recv, home, keep, side = {}, {}, {}, {}, {}
+    near, far, mid, outer, partner = {}, {}, {}, {}, {}
+    all_codes = [NEAR_CODES, FAR_CODES, MID_CODES, OUT_CODES]
+
+    def send_terms(i, served, *order):
+        sent, mark = matmul_send(here, lhs, rotation, columns[i], widths[i], *order)
+        core_recv[i] = lax.ppermute(sent, "hid", cores)
+        return served, mark
+
+    def keep_terms(i, served, *order):
+        recv = core_recv.pop(i)
+        away, home[i], mark = matmul_keep(here, lhs, rotation, recv, columns[i], widths[i], *order)
+        x_recv[i] = lax.ppermute(away, "hid", along_x)
+        return served, mark
+
+    def sum_terms(i, served, *order):
+        pieces = (experts, KINDS, block_rows, widths[i] // 2)
+        out, own, mark = add(here, home.pop(i), x_recv.pop(i), *order)
+        keep[i] = own.reshape(pieces)
+        side[i] = lax.ppermute(out.reshape(pieces), "ep", along_y)
+        return served, mark
+
+    def send_inward(i, served, *order):
+        near[i], mark = pack(keep.pop(i), side.pop(i), *order)
+        far[i] = lax.ppermute(near[i], "ep", inward)
+        return served, mark
+
+    def send_across(i, served, *order):
+        codes = [NEAR_CODES, FAR_CODES]
+        out, mark = pick(table, [near[i], far[i]], codes, AT_MID, LINK_CAP, *order)
+        mid[i] = lax.ppermute(out, "ep", middle)
+        return served, mark
+
+    def send_outward(i, served, *order):
+        codes = [NEAR_CODES, MID_CODES]
+        out, mark = pick(table, [near[i], mid[i]], codes, AT_OUT, LINK_CAP, *order)
+        outer[i] = lax.ppermute(out, "ep", outward)
+        return served, mark
+
+    def send_partner(i, served, *order):
+        sources = [near[i], far[i], mid[i], outer[i]]
+        out, mark = pick(table, sources, all_codes, AT_PARTNER, SLOT_TOTAL, *order)
+        partner[i] = lax.ppermute(out, "ep", along_y)
+        return served, mark
+
+    def put(i, served, *order):
+        sources = [near.pop(i), far.pop(i), mid.pop(i), outer.pop(i)]
+        return place(
+            here, table, sources, all_codes, partner.pop(i), columns[i], full_width, served, *order
+        )
+
+    stages = dict(
+        S=send_terms,
+        K=keep_terms,
+        A=sum_terms,
+        I=send_inward,
+        M=send_across,
+        O=send_outward,
+        P=send_partner,
+        L=put,
+    )
+    served, mark = None, here
+    for step in ORDER:
+        served, mark = stages[step[0]](int(step[1:]), served, mark, COST)
+    return served.transpose(1, 0, 2)[None]
 
 
 def count_below(bound, residue, shard_total):
@@ -32,7 +589,7 @@
     return chosen.reshape(1, slot_blocks * chosen.shape[1], chosen.shape[2], chosen.shape[3])
 
 
-def on_device(gate_proj, up_proj, down_proj, rotation, placement, row_count):
+def gathered(gate_proj, up_proj, down_proj, rotation, placement, row_count):
     shard_total = lax.axis_size("hid")
     owner_total = lax.axis_size("ep")
     experts, width_part, local_rows = gate_proj.shape
@@ -91,6 +648,11 @@
         P(),
     )
     out_specs = P("ep", "hid", None, None)
+    fits = mesh.shape["hid"] == 4 and mesh.shape["ep"] == 8
     return jax.shard_map(
-        on_device, mesh=mesh, in_specs=in_specs, out_specs=out_specs, check_vma=False
-    )
+        pipelined if fits else gathered,
+        mesh=mesh,
+        in_specs=in_specs,
+        out_specs=out_specs,
+        check_vma=False,
+    )

time: 1130 us -> 404 us (0.36)
  waiting for transfers between devices: 984 us -> 138 us
  Pallas kernels: 0 us -> 133 us
  starting transfers between devices: 0.04 us -> 107 us
  matrix products: 46.1 us -> 0 us
  local copies, waits for them, and re-layouts: 60.1 us -> 21.3 us
  other arithmetic: 15.7 us -> 0.07 us
  between operations: 14.2 us -> 1.48 us
  blocking collectives: 11.5 us -> 0 us
    all_gather x1 -> x0, waiting for transfers between devices: 821 us -> none  [on_device(): lax.all_gather(rotated[None], 'ep', axis=0, tiled=True)]
    reduce_scatter x1 -> x0, waiting for transfers between devices: 163 us -> none  [on_device(): lax.psum_scatter(jnp.einsum('fck,kh->fch', stacked, rotation, preferred_e...]
    ppermute x0 -> x63, waiting for transfers between devices: none -> 138 us  [the longest x9 47.3 us: send_partner(): partner[i] = lax.ppermute(out, 'ep', along_y)]
    pallas_call x0 -> x74, Pallas kernels: none -> 133 us  [the longest x9 33.6 us: matmul_keep(): pl.pallas_call(keep_kernel, out_shape=(out, out, MARK), grid_spec=pltpu.P...]
    ppermute x0 -> x63, starting transfers between devices: none -> 107 us  [the longest x9 48.6 us: send_inward(): far[i] = lax.ppermute(near[i], 'ep', inward)]
    gather x3 -> x0, local copies, waits for them, and re-layouts: 50.4 us -> none  [assemble(): chosen = received[source_ids, :, expert_ids]]
    dot_general x1 -> x0, matrix products: 46.1 us -> none  [on_device(): jnp.einsum('fck,kh->fch', stacked, rotation, preferred_element_type=jnp.f...]
    unnamed x13 -> x60, local copies, waits for them, and re-layouts: 9.21 us -> 21.3 us
  transfers between devices with their start and end apart: 2 -> 63, of which waited for: 2 -> 22; matrix products, arithmetic and copies ran while one was open for 0% -> 0% of each run, Pallas kernels for 0% -> 31%
where the time goes in v1:
time: 404 us; the launch traced here: 401 us
  waiting for transfers between devices  138 us (34%)
  Pallas kernels  133 us (33%)
  starting transfers between devices  107 us (26%)
  local copies, waits for them, and re-layouts  21.3 us (5%)
    ppermute x9, starting transfers between devices, send_inward(): far[i] = lax.ppermute(near[i], 'ep', inward)  48.6 us
    ppermute x9, waiting for transfers between devices, send_partner(): partner[i] = lax.ppermute(out, 'ep', along_y)  47.3 us
    ppermute x9, waiting for transfers between devices, send_outward(): outer[i] = lax.ppermute(out, 'ep', outward)  40.1 us
    pallas_call x9, Pallas kernels, matmul_keep(): pl.pallas_call(keep_kernel, out_shape=(out, out, MARK), grid_spec=pltpu.P...  33.6 us
    pallas_call x9, Pallas kernels, matmul_send(): pl.pallas_call(send_kernel, out_shape=(jax.ShapeDtypeStruct((rows, width)...  31.8 us
    pallas_call x27, Pallas kernels, pick(): pl.pallas_call(functools.partial(pick_kernel, first=first, bases=bases),...  31.3 us
    ppermute x9, waiting for transfers between devices, keep_terms(): x_recv[i] = lax.ppermute(away, 'hid', along_x)  28.8 us
    unnamed x60, local copies, waits for them, and re-layouts  21.3 us
  transfers between devices with their start and end apart: 63, of which 22 were waited for; matrix products, arithmetic and copies ran while one was open for 0% of the time, Pallas kernels for 31%

profile of v1, /device:TPU:0, one launch (start us, length us, event | category | flops | bytes accessed | tf_op | source)
XLA Modules:
  0.0 400.7 jit_solution(5242952048282775919)
XLA Ops:
  6.1 8.3 %copy-done.5 = bf16[1792,7168]{1,0:T(8,128)(2,1)S(1)} copy-done((bf16[1792,7168]{1,0:T(8,128)(2,1)S(1)}, bf16[1792,7168]{1,0:T(8,128)(2,1)}, u32[]{:S(2)}) %copy-start.5) | copy-done | bytes 25690136
  26.5 8.3 %copy-done.6 = bf16[1792,7168]{1,0:T(8,128)(2,1)S(1)} copy-done((bf16[1792,7168]{1,0:T(8,128)(2,1)S(1)}, bf16[1792,7168]{1,0:T(8,128)(2,1)}, u32[]{:S(2)}) %copy-start.6) | copy-done | bytes 25690136
  42.4 4.8 %matmul_keep.11 = (bf16[384,1024]{1,0:T(8,128)(2,1)S(1)}, bf16[384,1024]{1,0:T(8,128)(2,1)S(1)}, f32[8,128]{1,0:T(8,128)S(1)}) custom-call(s32[2]{0:T(128)S(1)} %pad_add_fusion.here_ref.after_ref, bf16[2,768,1792]{2,1,0:T(8,128)(2,1)S(1)} %bitcast.29, bf16[1792,7168]{1,0:T(8,128)(2,1)S(1)} %copy-done.6, bf16[1792,7168]{1,0:T(8,128)(2,1)S(1)} %copy-done.6, ...), custom_call_target="tpu_custom_call" | custom-call | flops 20000000000 | bytes 1024 | tf_op jit(solution)/shard_map/matmul_keep/pallas_call | solution.py:299
  47.2 13.3 %collective-permute-done.1.recv_ref = bf16[384,512]{1,0:T(8,128)(2,1)S(1)} collective-permute-done((bf16[384,512]{1,0:T(8,128)(2,1)S(1)}, bf16[384,512]{1,0:T(8,128)(2,1)S(1)}, u32[]{:S(2)}, u32[]{:S(2)}) %collective-permute-start.1) | collective-permute-done | bytes 393248 | tf_op jit(solution)/shard_map/ppermute | solution.py:509
  74.3 4.8 %matmul_keep.12 = (bf16[384,1024]{1,0:T(8,128)(2,1)S(1)}, bf16[384,1024]{1,0:T(8,128)(2,1)S(1)}, f32[8,128]{1,0:T(8,128)S(1)}) custom-call(s32[2]{0:T(128)S(1)} %pad_add_fusion.here_ref.after_ref, bf16[2,768,1792]{2,1,0:T(8,128)(2,1)S(1)} %bitcast.31, bf16[1792,7168]{1,0:T(8,128)(2,1)S(1)} %copy-done.6, bf16[1792,7168]{1,0:T(8,128)(2,1)S(1)} %copy-done.6, ...), custom_call_target="tpu_custom_call" | custom-call | flops 20000000000 | bytes 1024 | tf_op jit(solution)/shard_map/matmul_keep/pallas_call | solution.py:299
  96.1 5.8 %collective-permute-start.16 = (bf16[4,3,64,512]{3,2,1,0:T(8,128)(2,1)S(1)}, bf16[4,3,64,512]{3,2,1,0:T(8,128)(2,1)S(1)}, u32[]{:S(2)}, u32[]{:S(2)}) collective-permute-start(bf16[4,3,64,512]{3,2,1,0:T(8,128)(2,1)S(1)} %get-tuple-element.209.refs_0_), channel_id=1, source_target_pairs={{0,2},{1,3},{6,4},{7,5},{8,10},{9,11},{14,12},{15,13},{16,18},{17,... | collective-permute-start | bytes 2359304 | tf_op jit(solution)/shard_map/ppermute | solution.py:521
  102.7 4.8 %matmul_keep.13 = (bf16[384,1024]{1,0:T(8,128)(2,1)S(1)}, bf16[384,1024]{1,0:T(8,128)(2,1)S(1)}, f32[8,128]{1,0:T(8,128)S(1)}) custom-call(s32[2]{0:T(128)S(1)} %pad_add_fusion.here_ref.after_ref, bf16[2,768,1792]{2,1,0:T(8,128)(2,1)S(1)} %bitcast.33, bf16[1792,7168]{1,0:T(8,128)(2,1)S(1)} %copy-done.6, bf16[1792,7168]{1,0:T(8,128)(2,1)S(1)} %copy-done.6, ...), custom_call_target="tpu_custom_call" | custom-call | flops 20000000000 | bytes 1024 | tf_op jit(solution)/shard_map/matmul_keep/pallas_call | solution.py:299
  112.5 6.7 %collective-permute-done.16.refs_1_ = bf16[4,3,64,512]{3,2,1,0:T(8,128)(2,1)S(1)} collective-permute-done((bf16[4,3,64,512]{3,2,1,0:T(8,128)(2,1)S(1)}, bf16[4,3,64,512]{3,2,1,0:T(8,128)(2,1)S(1)}, u32[]{:S(2)}, u32[]{:S(2)}) %collective-permute-start.16) | collective-permute-done | bytes 786464 | tf_op jit(solution)/shard_map/ppermute | solution.py:521
  125.5 5.7 %collective-permute-start.17 = (bf16[4,3,64,512]{3,2,1,0:T(8,128)(2,1)S(1)}, bf16[4,3,64,512]{3,2,1,0:T(8,128)(2,1)S(1)}, u32[]{:S(2)}, u32[]{:S(2)}) collective-permute-start(bf16[4,3,64,512]{3,2,1,0:T(8,128)(2,1)S(1)} %get-tuple-element.212.refs_0_), channel_id=1, source_target_pairs={{0,2},{1,3},{6,4},{7,5},{8,10},{9,11},{14,12},{15,13},{16,18},{17,... | collective-permute-start | bytes 2359304 | tf_op jit(solution)/shard_map/ppermute | solution.py:521
  135.7 8.4 %collective-permute-done.20.side_ref = bf16[2,3,64,512]{3,2,1,0:T(8,128)(2,1)S(1)} collective-permute-done((bf16[2,3,64,512]{3,2,1,0:T(8,128)(2,1)S(1)}, bf16[2,3,64,512]{3,2,1,0:T(8,128)(2,1)S(1)}, u32[]{:S(2)}, u32[]{:S(2)}) %collective-permute-start.20) | collective-permute-done | bytes 393248 | tf_op jit(solution)/shard_map/ppermute | solution.py:516
  182.4 4.8 %matmul_keep.15 = (bf16[384,1024]{1,0:T(8,128)(2,1)S(1)}, bf16[384,1024]{1,0:T(8,128)(2,1)S(1)}, f32[8,128]{1,0:T(8,128)S(1)}) custom-call(s32[2]{0:T(128)S(1)} %pad_add_fusion.here_ref.after_ref, bf16[2,768,1792]{2,1,0:T(8,128)(2,1)S(1)} %bitcast.37, bf16[1792,7168]{1,0:T(8,128)(2,1)S(1)} %copy-done.6, bf16[1792,7168]{1,0:T(8,128)(2,1)S(1)} %copy-done.6, ...), custom_call_target="tpu_custom_call" | custom-call | flops 20000000000 | bytes 1024 | tf_op jit(solution)/shard_map/matmul_keep/pallas_call | solution.py:299
  187.2 4.9 %collective-permute-done.28.recv_ref = bf16[384,1024]{1,0:T(8,128)(2,1)S(1)} collective-permute-done((bf16[384,1024]{1,0:T(8,128)(2,1)S(1)}, bf16[384,1024]{1,0:T(8,128)(2,1)S(1)}, u32[]{:S(2)}, u32[]{:S(2)}) %collective-permute-start.28) | collective-permute-done | bytes 786464 | tf_op jit(solution)/shard_map/ppermute | solution.py:509
  197.4 6.6 %collective-permute-done.32.refs_3_ = bf16[8,3,64,512]{3,2,1,0:T(8,128)(2,1)S(1)} collective-permute-done((bf16[8,3,64,512]{3,2,1,0:T(8,128)(2,1)S(1)}, bf16[8,3,64,512]{3,2,1,0:T(8,128)(2,1)S(1)}, u32[]{:S(2)}, u32[]{:S(2)}) %collective-permute-start.32) | collective-permute-done | bytes 1572896 | tf_op jit(solution)/shard_map/ppermute | solution.py:533
  208.5 5.8 %collective-permute-start.39 = (bf16[4,3,64,512]{3,2,1,0:T(8,128)(2,1)S(1)}, bf16[4,3,64,512]{3,2,1,0:T(8,128)(2,1)S(1)}, u32[]{:S(2)}, u32[]{:S(2)}) collective-permute-start(bf16[4,3,64,512]{3,2,1,0:T(8,128)(2,1)S(1)} %get-tuple-element.263.refs_0_), channel_id=1, source_target_pairs={{0,2},{1,3},{6,4},{7,5},{8,10},{9,11},{14,12},{15,13},{16,18},{17,... | collective-permute-start | bytes 2359304 | tf_op jit(solution)/shard_map/ppermute | solution.py:521
  215.7 10.0 %collective-permute-done.33.refs_4_ = bf16[4,3,64,512]{3,2,1,0:T(8,128)(2,1)S(1)} collective-permute-done((bf16[4,3,64,512]{3,2,1,0:T(8,128)(2,1)S(1)}, bf16[4,3,64,512]{3,2,1,0:T(8,128)(2,1)S(1)}, u32[]{:S(2)}, u32[]{:S(2)}) %collective-permute-start.33) | collective-permute-done | bytes 786464 | tf_op jit(solution)/shard_map/ppermute | solution.py:539
  259.1 7.9 %collective-permute-done.40.refs_4_ = bf16[4,3,64,512]{3,2,1,0:T(8,128)(2,1)S(1)} collective-permute-done((bf16[4,3,64,512]{3,2,1,0:T(8,128)(2,1)S(1)}, bf16[4,3,64,512]{3,2,1,0:T(8,128)(2,1)S(1)}, u32[]{:S(2)}, u32[]{:S(2)}) %collective-permute-start.40) | collective-permute-done | bytes 786464 | tf_op jit(solution)/shard_map/ppermute | solution.py:539
  272.6 7.5 %collective-permute-start.47 = (bf16[4,3,64,256]{3,2,1,0:T(8,128)(2,1)S(1)}, bf16[4,3,64,256]{3,2,1,0:T(8,128)(2,1)S(1)}, u32[]{:S(2)}, u32[]{:S(2)}) collective-permute-start(bf16[4,3,64,256]{3,2,1,0:T(8,128)(2,1)S(1)} %get-tuple-element.287.refs_0_), channel_id=1, source_target_pairs={{0,2},{1,3},{6,4},{7,5},{8,10},{9,11},{14,12},{15,13},{16,18},{17,... | collective-permute-start | bytes 1179656 | tf_op jit(solution)/shard_map/ppermute | solution.py:521
  290.1 6.2 %collective-permute-done.46.recv_ref = bf16[384,512]{1,0:T(8,128)(2,1)S(1)} collective-permute-done((bf16[384,512]{1,0:T(8,128)(2,1)S(1)}, bf16[384,512]{1,0:T(8,128)(2,1)S(1)}, u32[]{:S(2)}, u32[]{:S(2)}) %collective-permute-start.46) | collective-permute-done | bytes 393248 | tf_op jit(solution)/shard_map/ppermute | solution.py:509
  298.5 10.4 %collective-permute-done.51.refs_4_ = bf16[4,3,64,512]{3,2,1,0:T(8,128)(2,1)S(1)} collective-permute-done((bf16[4,3,64,512]{3,2,1,0:T(8,128)(2,1)S(1)}, bf16[4,3,64,512]{3,2,1,0:T(8,128)(2,1)S(1)}, u32[]{:S(2)}, u32[]{:S(2)}) %collective-permute-start.51) | collective-permute-done | bytes 786464 | tf_op jit(solution)/shard_map/ppermute | solution.py:539
  312.9 9.2 %collective-permute-start.52 = (bf16[4,3,64,256]{3,2,1,0:T(8,128)(2,1)S(1)}, bf16[4,3,64,256]{3,2,1,0:T(8,128)(2,1)S(1)}, u32[]{:S(2)}, u32[]{:S(2)}) collective-permute-start(bf16[4,3,64,256]{3,2,1,0:T(8,128)(2,1)S(1)} %get-tuple-element.300.refs_0_), channel_id=1, source_target_pairs={{0,2},{1,3},{6,4},{7,5},{8,10},{9,11},{14,12},{15,13},{16,18},{17,... | collective-permute-start | bytes 1179656 | tf_op jit(solution)/shard_map/ppermute | solution.py:521
  331.0 9.3 %collective-permute-done.55.refs_4_ = bf16[4,3,64,512]{3,2,1,0:T(8,128)(2,1)S(1)} collective-permute-done((bf16[4,3,64,512]{3,2,1,0:T(8,128)(2,1)S(1)}, bf16[4,3,64,512]{3,2,1,0:T(8,128)(2,1)S(1)}, u32[]{:S(2)}, u32[]{:S(2)}) %collective-permute-start.55) | collective-permute-done | bytes 786464 | tf_op jit(solution)/shard_map/ppermute | solution.py:539
  344.9 16.4 %collective-permute-done.59.refs_3_ = bf16[8,3,64,512]{3,2,1,0:T(8,128)(2,1)S(1)} collective-permute-done((bf16[8,3,64,512]{3,2,1,0:T(8,128)(2,1)S(1)}, bf16[8,3,64,512]{3,2,1,0:T(8,128)(2,1)S(1)}, u32[]{:S(2)}, u32[]{:S(2)}) %collective-permute-start.59) | collective-permute-done | bytes 1572896 | tf_op jit(solution)/shard_map/ppermute | solution.py:533
  363.7 14.5 %collective-permute-done.58.refs_3_ = bf16[8,3,64,256]{3,2,1,0:T(8,128)(2,1)S(1)} collective-permute-done((bf16[8,3,64,256]{3,2,1,0:T(8,128)(2,1)S(1)}, bf16[8,3,64,256]{3,2,1,0:T(8,128)(2,1)S(1)}, u32[]{:S(2)}, u32[]{:S(2)}) %collective-permute-start.58) | collective-permute-done | bytes 786464 | tf_op jit(solution)/shard_map/ppermute | solution.py:533
  392.8 5.8 %collective-permute-done.62.refs_4_ = bf16[4,3,64,256]{3,2,1,0:T(8,128)(2,1)S(1)} collective-permute-done((bf16[4,3,64,256]{3,2,1,0:T(8,128)(2,1)S(1)}, bf16[4,3,64,256]{3,2,1,0:T(8,128)(2,1)S(1)}, u32[]{:S(2)}, u32[]{:S(2)}) %collective-permute-start.62) | collective-permute-done | bytes 393248 | tf_op jit(solution)/shard_map/ppermute | solution.py:539
  (237 shorter events, 209.0 us)
Async XLA Ops:
  39.7 29.3 %collective-permute-start.6 = (bf16[384,512]{1,0:T(8,128)(2,1)S(1)}, bf16[384,512]{1,0:T(8,128)(2,1)S(1)}, u32[]{:S(2)}, u32[]{:S(2)}) collective-permute-start(bf16[384,512]{1,0:T(8,128)(2,1)S(1)} %get-tuple-element.182), channel_id=1, source_target_pairs={{0,16},{8,24},{16,0},{24,8},{1,17},{9,25},{17,1},{25,9},{2,18},{10... | collective-permute-start | bytes 1179656 | tf_op jit(solution)/shard_map/ppermute | solution.py:509
  63.0 21.5 %collective-permute-start.11 = (bf16[384,1024]{1,0:T(8,128)(2,1)S(1)}, bf16[384,1024]{1,0:T(8,128)(2,1)S(1)}, u32[]{:S(2)}, u32[]{:S(2)}) collective-permute-start(bf16[384,1024]{1,0:T(8,128)(2,1)S(1)} %get-tuple-element.195), channel_id=1, source_target_pairs={{0,16},{8,24},{16,0},{24,8},{1,17},{9,25},{17,1},{25,9},{2,18},{10... | collective-permute-start | bytes 2359304 | tf_op jit(solution)/shard_map/ppermute | solution.py:509
  96.1 23.1 %collective-permute-start.16 = (bf16[4,3,64,512]{3,2,1,0:T(8,128)(2,1)S(1)}, bf16[4,3,64,512]{3,2,1,0:T(8,128)(2,1)S(1)}, u32[]{:S(2)}, u32[]{:S(2)}) collective-permute-start(bf16[4,3,64,512]{3,2,1,0:T(8,128)(2,1)S(1)} %get-tuple-element.209.refs_0_), channel_id=1, source_target_pairs={{0,2},{1,3},{6,4},{7,5},{8,10},{9,11},{14,12},{15,13},{16,18},{17,... | collective-permute-start | bytes 2359304 | tf_op jit(solution)/shard_map/ppermute | solution.py:521
  101.9 21.4 %collective-permute-start.19 = (bf16[8,3,64,256]{3,2,1,0:T(8,128)(2,1)S(1)}, bf16[8,3,64,256]{3,2,1,0:T(8,128)(2,1)S(1)}, u32[]{:S(2)}, u32[]{:S(2)}) collective-permute-start(bf16[8,3,64,256]{3,2,1,0:T(8,128)(2,1)S(1)} %get-tuple-element.215), channel_id=1, source_target_pairs={{2,4},{3,5},{4,2},{5,3},{10,12},{11,13},{12,10},{13,11},{18,20},{1... | collective-permute-start | bytes 2359304 | tf_op jit(solution)/shard_map/ppermute | solution.py:527
  109.6 23.2 %collective-permute-start.21 = (bf16[8,3,64,256]{3,2,1,0:T(8,128)(2,1)S(1)}, bf16[8,3,64,256]{3,2,1,0:T(8,128)(2,1)S(1)}, u32[]{:S(2)}, u32[]{:S(2)}) collective-permute-start(bf16[8,3,64,256]{3,2,1,0:T(8,128)(2,1)S(1)} %get-tuple-element.220), channel_id=1, source_target_pairs={{4,6},{5,7},{2,0},{3,1},{12,14},{13,15},{10,8},{11,9},{20,22},{21,... | collective-permute-start | bytes 2359304 | tf_op jit(solution)/shard_map/ppermute | solution.py:533
  121.1 41.7 %collective-permute-start.27 = (bf16[8,3,64,512]{3,2,1,0:T(8,128)(2,1)}, bf16[8,3,64,512]{3,2,1,0:T(8,128)(2,1)}, u32[]{:S(2)}, u32[]{:S(2)}) collective-permute-start(bf16[8,3,64,512]{3,2,1,0:T(8,128)(2,1)} %get-tuple-element.232), channel_id=1, source_target_pairs={{2,4},{3,5},{4,2},{5,3},{10,12},{11,13},{12,10},{13,11},{18,20},{1... | collective-permute-start | bytes 4718600 | tf_op jit(solution)/shard_map/ppermute | solution.py:527
  124.2 27.8 %collective-permute-start.24 = (bf16[8,3,64,256]{3,2,1,0:T(8,128)(2,1)S(1)}, bf16[8,3,64,256]{3,2,1,0:T(8,128)(2,1)S(1)}, u32[]{:S(2)}, u32[]{:S(2)}) collective-permute-start(bf16[8,3,64,256]{3,2,1,0:T(8,128)(2,1)S(1)} %get-tuple-element.226), channel_id=1, source_target_pairs={{4,6},{5,7},{2,0},{3,1},{12,14},{13,15},{10,8},{11,9},{20,22},{21,... | collective-permute-start | bytes 2359304 | tf_op jit(solution)/shard_map/ppermute | solution.py:533
  125.5 24.4 %collective-permute-start.17 = (bf16[4,3,64,512]{3,2,1,0:T(8,128)(2,1)S(1)}, bf16[4,3,64,512]{3,2,1,0:T(8,128)(2,1)S(1)}, u32[]{:S(2)}, u32[]{:S(2)}) collective-permute-start(bf16[4,3,64,512]{3,2,1,0:T(8,128)(2,1)S(1)} %get-tuple-element.212.refs_0_), channel_id=1, source_target_pairs={{0,2},{1,3},{6,4},{7,5},{8,10},{9,11},{14,12},{15,13},{16,18},{17,... | collective-permute-start | bytes 2359304 | tf_op jit(solution)/shard_map/ppermute | solution.py:521
  133.8 22.4 %collective-permute-start.23 = (bf16[4,3,64,256]{3,2,1,0:T(8,128)(2,1)S(1)}, bf16[4,3,64,256]{3,2,1,0:T(8,128)(2,1)S(1)}, u32[]{:S(2)}, u32[]{:S(2)}) collective-permute-start(bf16[4,3,64,256]{3,2,1,0:T(8,128)(2,1)S(1)} %get-tuple-element.225), channel_id=1, source_target_pairs={{0,1},{1,0},{2,3},{3,2},{4,5},{5,4},{6,7},{7,6},{8,9},{9,8},{10,11... | collective-permute-start | bytes 1179656 | tf_op jit(solution)/shard_map/ppermute | solution.py:539
  145.5 33.2 %collective-permute-start.30 = (bf16[4,3,64,512]{3,2,1,0:T(8,128)(2,1)}, bf16[4,3,64,512]{3,2,1,0:T(8,128)(2,1)}, u32[]{:S(2)}, u32[]{:S(2)}) collective-permute-start(bf16[4,3,64,512]{3,2,1,0:T(8,128)(2,1)} %get-tuple-element.241.refs_0_), channel_id=1, source_target_pairs={{0,2},{1,3},{6,4},{7,5},{8,10},{9,11},{14,12},{15,13},{16,18},{17,... | collective-permute-start | bytes 2359304 | tf_op jit(solution)/shard_map/ppermute | solution.py:521
  154.4 41.0 %collective-permute-start.22 = (bf16[8,3,64,512]{3,2,1,0:T(8,128)(2,1)}, bf16[8,3,64,512]{3,2,1,0:T(8,128)(2,1)}, u32[]{:S(2)}, u32[]{:S(2)}) collective-permute-start(bf16[8,3,64,512]{3,2,1,0:T(8,128)(2,1)} %get-tuple-element.224), channel_id=1, source_target_pairs={{2,4},{3,5},{4,2},{5,3},{10,12},{11,13},{12,10},{13,11},{18,20},{1... | collective-permute-start | bytes 4718600 | tf_op jit(solution)/shard_map/ppermute | solution.py:527
  163.6 40.4 %collective-permute-start.32 = (bf16[8,3,64,512]{3,2,1,0:T(8,128)(2,1)S(1)}, bf16[8,3,64,512]{3,2,1,0:T(8,128)(2,1)S(1)}, u32[]{:S(2)}, u32[]{:S(2)}) collective-permute-start(bf16[8,3,64,512]{3,2,1,0:T(8,128)(2,1)S(1)} %get-tuple-element.247), channel_id=1, source_target_pairs={{4,6},{5,7},{2,0},{3,1},{12,14},{13,15},{10,8},{11,9},{20,22},{21,... | collective-permute-start | bytes 4718600 | tf_op jit(solution)/shard_map/ppermute | solution.py:533
  180.5 56.7 %collective-permute-start.37 = (bf16[8,3,64,512]{3,2,1,0:T(8,128)(2,1)}, bf16[8,3,64,512]{3,2,1,0:T(8,128)(2,1)}, u32[]{:S(2)}, u32[]{:S(2)}) collective-permute-start(bf16[8,3,64,512]{3,2,1,0:T(8,128)(2,1)} %get-tuple-element.260), channel_id=1, source_target_pairs={{2,4},{3,5},{4,2},{5,3},{10,12},{11,13},{12,10},{13,11},{18,20},{1... | collective-permute-start | bytes 4718600 | tf_op jit(solution)/shard_map/ppermute | solution.py:527
  206.8 39.5 %collective-permute-start.31 = (bf16[8,3,64,512]{3,2,1,0:T(8,128)(2,1)}, bf16[8,3,64,512]{3,2,1,0:T(8,128)(2,1)}, u32[]{:S(2)}, u32[]{:S(2)}) collective-permute-start(bf16[8,3,64,512]{3,2,1,0:T(8,128)(2,1)} %get-tuple-element.246), channel_id=1, source_target_pairs={{4,6},{5,7},{2,0},{3,1},{12,14},{13,15},{10,8},{11,9},{20,22},{21,... | collective-permute-start | bytes 4718600 | tf_op jit(solution)/shard_map/ppermute | solution.py:533
  208.5 22.3 %collective-permute-start.39 = (bf16[4,3,64,512]{3,2,1,0:T(8,128)(2,1)S(1)}, bf16[4,3,64,512]{3,2,1,0:T(8,128)(2,1)S(1)}, u32[]{:S(2)}, u32[]{:S(2)}) collective-permute-start(bf16[4,3,64,512]{3,2,1,0:T(8,128)(2,1)S(1)} %get-tuple-element.263.refs_0_), channel_id=1, source_target_pairs={{0,2},{1,3},{6,4},{7,5},{8,10},{9,11},{14,12},{15,13},{16,18},{17,... | collective-permute-start | bytes 2359304 | tf_op jit(solution)/shard_map/ppermute | solution.py:521
  233.5 21.8 %collective-permute-start.41 = (bf16[4,3,64,512]{3,2,1,0:T(8,128)(2,1)S(1)}, bf16[4,3,64,512]{3,2,1,0:T(8,128)(2,1)S(1)}, u32[]{:S(2)}, u32[]{:S(2)}) collective-permute-start(bf16[4,3,64,512]{3,2,1,0:T(8,128)(2,1)S(1)} %get-tuple-element.270.refs_0_), channel_id=1, source_target_pairs={{0,2},{1,3},{6,4},{7,5},{8,10},{9,11},{14,12},{15,13},{16,18},{17,... | collective-permute-start | bytes 2359304 | tf_op jit(solution)/shard_map/ppermute | solution.py:521
  239.1 46.2 %collective-permute-start.48 = (bf16[8,3,64,512]{3,2,1,0:T(8,128)(2,1)}, bf16[8,3,64,512]{3,2,1,0:T(8,128)(2,1)}, u32[]{:S(2)}, u32[]{:S(2)}) collective-permute-start(bf16[8,3,64,512]{3,2,1,0:T(8,128)(2,1)} %get-tuple-element.288), channel_id=1, source_target_pairs={{4,6},{5,7},{2,0},{3,1},{12,14},{13,15},{10,8},{11,9},{20,22},{21,... | collective-permute-start | bytes 4718600 | tf_op jit(solution)/shard_map/ppermute | solution.py:533
  240.4 39.8 %collective-permute-start.44 = (bf16[8,3,64,512]{3,2,1,0:T(8,128)(2,1)S(1)}, bf16[8,3,64,512]{3,2,1,0:T(8,128)(2,1)S(1)}, u32[]{:S(2)}, u32[]{:S(2)}) collective-permute-start(bf16[8,3,64,512]{3,2,1,0:T(8,128)(2,1)S(1)} %get-tuple-element.279), channel_id=1, source_target_pairs={{2,4},{3,5},{4,2},{5,3},{10,12},{11,13},{12,10},{13,11},{18,20},{1... | collective-permute-start | bytes 4718600 | tf_op jit(solution)/shard_map/ppermute | solution.py:527
  257.3 54.4 %collective-permute-start.50 = (bf16[8,3,64,512]{3,2,1,0:T(8,128)(2,1)}, bf16[8,3,64,512]{3,2,1,0:T(8,128)(2,1)}, u32[]{:S(2)}, u32[]{:S(2)}) collective-permute-start(bf16[8,3,64,512]{3,2,1,0:T(8,128)(2,1)} %get-tuple-element.294), channel_id=1, source_target_pairs={{2,4},{3,5},{4,2},{5,3},{10,12},{11,13},{12,10},{13,11},{18,20},{1... | collective-permute-start | bytes 4718600 | tf_op jit(solution)/shard_map/ppermute | solution.py:527
  281.0 42.5 %collective-permute-start.53 = (bf16[8,3,64,512]{3,2,1,0:T(8,128)(2,1)S(1)}, bf16[8,3,64,512]{3,2,1,0:T(8,128)(2,1)S(1)}, u32[]{:S(2)}, u32[]{:S(2)}) collective-permute-start(bf16[8,3,64,512]{3,2,1,0:T(8,128)(2,1)S(1)} %get-tuple-element.301), channel_id=1, source_target_pairs={{4,6},{5,7},{2,0},{3,1},{12,14},{13,15},{10,8},{11,9},{20,22},{21,... | collective-permute-start | bytes 4718600 | tf_op jit(solution)/shard_map/ppermute | solution.py:533
  287.7 40.5 %collective-permute-start.56 = (bf16[8,3,64,256]{3,2,1,0:T(8,128)(2,1)S(1)}, bf16[8,3,64,256]{3,2,1,0:T(8,128)(2,1)S(1)}, u32[]{:S(2)}, u32[]{:S(2)}) collective-permute-start(bf16[8,3,64,256]{3,2,1,0:T(8,128)(2,1)S(1)} %get-tuple-element.306), channel_id=1, source_target_pairs={{2,4},{3,5},{4,2},{5,3},{10,12},{11,13},{12,10},{13,11},{18,20},{1... | collective-permute-start | bytes 2359304 | tf_op jit(solution)/shard_map/ppermute | solution.py:527
  322.1 39.2 %collective-permute-start.59 = (bf16[8,3,64,512]{3,2,1,0:T(8,128)(2,1)S(1)}, bf16[8,3,64,512]{3,2,1,0:T(8,128)(2,1)S(1)}, u32[]{:S(2)}, u32[]{:S(2)}) collective-permute-start(bf16[8,3,64,512]{3,2,1,0:T(8,128)(2,1)S(1)} %get-tuple-element.313), channel_id=1, source_target_pairs={{4,6},{5,7},{2,0},{3,1},{12,14},{13,15},{10,8},{11,9},{20,22},{21,... | collective-permute-start | bytes 4718600 | tf_op jit(solution)/shard_map/ppermute | solution.py:533
  329.0 49.3 %collective-permute-start.58 = (bf16[8,3,64,256]{3,2,1,0:T(8,128)(2,1)S(1)}, bf16[8,3,64,256]{3,2,1,0:T(8,128)(2,1)S(1)}, u32[]{:S(2)}, u32[]{:S(2)}) collective-permute-start(bf16[8,3,64,256]{3,2,1,0:T(8,128)(2,1)S(1)} %get-tuple-element.312), channel_id=1, source_target_pairs={{4,6},{5,7},{2,0},{3,1},{12,14},{13,15},{10,8},{11,9},{20,22},{21,... | collective-permute-start | bytes 2359304 | tf_op jit(solution)/shard_map/ppermute | solution.py:533
  343.6 45.7 %collective-permute-start.57 = (bf16[8,3,64,256]{3,2,1,0:T(8,128)(2,1)S(1)}, bf16[8,3,64,256]{3,2,1,0:T(8,128)(2,1)S(1)}, u32[]{:S(2)}, u32[]{:S(2)}) collective-permute-start(bf16[8,3,64,256]{3,2,1,0:T(8,128)(2,1)S(1)} %get-tuple-element.311), channel_id=1, source_target_pairs={{4,6},{5,7},{2,0},{3,1},{12,14},{13,15},{10,8},{11,9},{20,22},{21,... | collective-permute-start | bytes 2359304 | tf_op jit(solution)/shard_map/ppermute | solution.py:533
  (69 other events, 752.4 us)

commit v2 on v1

--- a/solution.py
+++ b/solution.py
@@ -10,12 +10,12 @@
 CHUNK_TILES = (1, 1, 2, 2, 2, 2, 2, 1, 1)
 MATMUL_VMEM = 16 * 2**20
 MOVE_VMEM = 8 * 2**20
-COST = pl.CostEstimate(flops=20000000000, bytes_accessed=2**10, transcendentals=0)
+COST = pl.CostEstimate(flops=25000000000, bytes_accessed=2**10, transcendentals=0)
 ORDER = (
     'S0',
+    'K0',
     'S1',
     'S2',
-    'K0',
     'K1',
     'K2',
     'A0',
@@ -81,8 +81,8 @@
     'P6',
     'P7',
     'L6',
+    'P8',
     'L7',
-    'P8',
     'L8',
 )
 MARK = jax.ShapeDtypeStruct((8, 128), jnp.float32)
@@ -195,7 +195,8 @@
 ANYWHERE = pl.BlockSpec(memory_space=pl.ANY)
 ON_SMEM = pl.BlockSpec(memory_space=pltpu.SMEM)
 ON_VMEM = pl.BlockSpec(memory_space=pltpu.VMEM)
-TILE = 512
+ON_HBM = pl.BlockSpec(memory_space=pltpu.HBM)
+TILE = 256
 
 
 def gather_rows_kernel(gate_ref, up_ref, down_ref, out_ref):
@@ -227,23 +228,39 @@
     return rows.reshape(2, 2 * experts * KINDS * block_rows, depth)
 
 
-def product(lhs_ref, top_ref, bottom_ref):
-    depth = top_ref.shape[0]
+def product(here_ref, lhs_ref, rot_ref, tile_ref, sems, column):
+    step, total = pl.program_id(0), pl.num_programs(0)
+
+    def tile_copy(index):
+        slot = lax.rem(index, 2)
+        columns = pl.ds(pl.multiple_of(column + index * TILE, TILE), TILE)
+        return pltpu.make_async_copy(rot_ref.at[:, columns], tile_ref.at[slot], sems.at[slot])
+
+    @pl.when(step == 0)
+    def _():
+        tile_copy(step).start()
+
+    @pl.when(step + 1 < total)
+    def _():
+        tile_copy(step + 1).start()
+
+    tile_copy(step).wait()
     return jnp.dot(
-        lhs_ref[0, :, :depth], top_ref[...], preferred_element_type=jnp.float32
-    ) + jnp.dot(lhs_ref[0, :, depth:], bottom_ref[...], preferred_element_type=jnp.float32)
-
-
-def send_kernel(here_ref, lhs_ref, top_ref, bottom_ref, after_ref, out_ref, mark_ref):
-    out_ref[...] = product(lhs_ref, top_ref, bottom_ref).astype(jnp.bfloat16)
+        lhs_ref[0], tile_ref[lax.rem(step, 2)], preferred_element_type=jnp.float32
+    )
+
+
+def send_kernel(here_ref, lhs_ref, rot_ref, after_ref, out_ref, mark_ref, *scratch, column):
+    total = product(here_ref, lhs_ref, rot_ref, *scratch, column)
+    out_ref[...] = total.astype(jnp.bfloat16)
 
 
 def keep_kernel(
-    here_ref, lhs_ref, top_ref, bottom_ref, recv_ref, after_ref, away_ref, home_ref, mark_ref
+    here_ref, lhs_ref, rot_ref, recv_ref, after_ref, away_ref, home_ref, mark_ref, *scratch, column
 ):
     rows = away_ref.shape[0]
-    total = product(lhs_ref, top_ref, bottom_ref) + recv_ref[...].astype(jnp.float32)
-    total = total.astype(jnp.bfloat16)
+    total = product(here_ref, lhs_ref, rot_ref, *scratch, column)
+    total = (total + recv_ref[...].astype(jnp.float32)).astype(jnp.bfloat16)
     x = here_ref[0] // 2
 
     @pl.when(x == 0)
@@ -257,58 +274,57 @@
         away_ref[...] = total[:rows]
 
 
-def matmul_specs(lhs, column, send):
+def lhs_spec(lhs, send):
     _, rows, depth = lhs.shape
 
     def lhs_map(tile, here):
         core = here[0] % 2
         return (1 - core if send else core, 0, 0)
 
-    def rot_map(part, tile, here):
-        return (part, column // TILE + tile)
-
-    return [
-        pl.BlockSpec((1, rows, depth), lhs_map, pipeline_mode=pl.Buffered(1)),
-        pl.BlockSpec((depth // 2, TILE), functools.partial(rot_map, 0)),
-        pl.BlockSpec((depth // 2, TILE), functools.partial(rot_map, 1)),
-    ]
+    return pl.BlockSpec((1, rows, depth), lhs_map, pipeline_mode=pl.Buffered(1))
+
+
+def tile_scratch(depth):
+    return [pltpu.VMEM((2, depth, TILE), jnp.bfloat16), pltpu.SemaphoreType.DMA((2,))]
 
 
 def matmul_send(here, lhs, rotation, column, width, after, cost):
-    _, rows, _ = lhs.shape
+    _, rows, depth = lhs.shape
     return pl.pallas_call(
-        send_kernel,
+        functools.partial(send_kernel, column=column),
         out_shape=(jax.ShapeDtypeStruct((rows, width), jnp.bfloat16), MARK),
         grid_spec=pltpu.PrefetchScalarGridSpec(
             num_scalar_prefetch=1,
             grid=(width // TILE,),
-            in_specs=matmul_specs(lhs, column, True) + [ANYWHERE],
+            in_specs=[lhs_spec(lhs, True), ON_HBM, ANYWHERE],
             out_specs=(pl.BlockSpec((rows, TILE), lambda t, here: (0, t)), ANYWHERE),
+            scratch_shapes=tile_scratch(depth),
         ),
         compiler_params=pltpu.CompilerParams(vmem_limit_bytes=MATMUL_VMEM),
         cost_estimate=cost,
         name="matmul_send",
-    )(here, lhs, rotation, rotation, after)
+    )(here, lhs, rotation, after)
 
 
 def matmul_keep(here, lhs, rotation, recv, column, width, after, cost):
-    _, rows, _ = lhs.shape
+    _, rows, depth = lhs.shape
     out = jax.ShapeDtypeStruct((rows // 2, width), jnp.bfloat16)
     out_spec = pl.BlockSpec((rows // 2, TILE), lambda t, here: (0, t))
     recv_spec = pl.BlockSpec((rows, TILE), lambda t, here: (0, t))
     return pl.pallas_call(
-        keep_kernel,
+        functools.partial(keep_kernel, column=column),
         out_shape=(out, out, MARK),
         grid_spec=pltpu.PrefetchScalarGridSpec(
             num_scalar_prefetch=1,
             grid=(width // TILE,),
-            in_specs=matmul_specs(lhs, column, False) + [recv_spec, ANYWHERE],
+            in_specs=[lhs_spec(lhs, False), ON_HBM, recv_spec, ANYWHERE],
             out_specs=(out_spec, out_spec, ANYWHERE),
+            scratch_shapes=tile_scratch(depth),
         ),
         compiler_params=pltpu.CompilerParams(vmem_limit_bytes=MATMUL_VMEM),
         cost_estimate=cost,
         name="matmul_keep",
-    )(here, lhs, rotation, rotation, recv, after)
+    )(here, lhs, rotation, recv, after)
 
 
 def add_kernel(here_ref, home_ref, recv_ref, after_ref, side_ref, keep_ref, mark_ref):
@@ -490,7 +506,7 @@
     inward = [(0, 2), (1, 3), (6, 4), (7, 5)]
     middle = [(2, 4), (3, 5), (4, 2), (5, 3)]
     outward = [(4, 6), (5, 7), (2, 0), (3, 1)]
-    widths = [tiles * TILE for tiles in CHUNK_TILES]
+    widths = [2 * tiles * TILE for tiles in CHUNK_TILES]
     columns = [sum(widths[:i]) for i in range(len(widths))]
     chunks = len(widths)
 

time: 404 us -> 407 us (level)
  Pallas kernels: 133 us -> 149 us
  waiting for transfers between devices: 138 us -> 130 us
    ppermute x9, waiting for transfers between devices: 28.8 us -> 18.3 us  [keep_terms(): x_recv[i] = lax.ppermute(away, 'hid', along_x)]
    pallas_call x18, Pallas kernels: 65.4 us -> 73.1 us  [the longest x9 38.2 us: matmul_keep(): pl.pallas_call(functools.partial(keep_kernel, column=column), out_shape=(...]
    ppermute x9, waiting for transfers between devices: 40.1 us -> 47.1 us  [send_outward(): outer[i] = lax.ppermute(out, 'ep', outward)]
    ppermute x9, starting transfers between devices: 13.4 us -> 7.42 us  [send_partner(): partner[i] = lax.ppermute(out, 'ep', along_y)]
    unnamed x60 -> x36, local copies, waits for them, and re-layouts: 21.3 us -> 21.7 us
  transfers between devices with their start and end apart: 63 -> 63, of which waited for: 22 -> 21; matrix products, arithmetic and copies ran while one was open for 0% -> 0% of each run, Pallas kernels for 31% -> 34%
where the time goes in v2:
time: 407 us
  Pallas kernels  149 us (37%)
  waiting for transfers between devices  130 us (32%)
  starting transfers between devices  105 us (26%)
  local copies, waits for them, and re-layouts  21.7 us (5%)
    ppermute x9, starting transfers between devices, send_inward(): far[i] = lax.ppermute(near[i], 'ep', inward)  51 us
    ppermute x9, waiting for transfers between devices, send_outward(): outer[i] = lax.ppermute(out, 'ep', outward)  47.1 us
    ppermute x9, waiting for transfers between devices, send_partner(): partner[i] = lax.ppermute(out, 'ep', along_y)  43.9 us
    pallas_call x9, Pallas kernels, matmul_keep(): pl.pallas_call(functools.partial(keep_kernel, column=column), out_shape=(...  38.2 us
    pallas_call x27, Pallas kernels, pick(): pl.pallas_call(functools.partial(pick_kernel, first=first, bases=bases),...  35.2 us
    pallas_call x9, Pallas kernels, matmul_send(): pl.pallas_call(functools.partial(send_kernel, column=column), out_shape=(...  34.9 us
    pallas_call x9, Pallas kernels, place(): pl.pallas_call(functools.partial(place_kernel, bases=bases, column=column...  23.6 us
    unnamed x36, local copies, waits for them, and re-layouts  21.7 us
  transfers between devices with their start and end apart: 63, of which 21 were waited for; matrix products, arithmetic and copies ran while one was open for 0% of the time, Pallas kernels for 34%

profile of v2, /device:TPU:0, one launch (start us, length us, event | category | flops | bytes accessed | tf_op | source)
XLA Modules:
  0.0 407.2 jit_solution(7476777439418644159)
XLA Ops:
  6.1 8.3 %copy-done.5 = bf16[1792,7168]{1,0:T(8,128)(2,1)S(1)} copy-done((bf16[1792,7168]{1,0:T(8,128)(2,1)S(1)}, bf16[1792,7168]{1,0:T(8,128)(2,1)}, u32[]{:S(2)}) %copy-start.5) | copy-done | bytes 25690136
  19.5 8.3 %copy-done.6 = bf16[1792,7168]{1,0:T(8,128)(2,1)S(1)} copy-done((bf16[1792,7168]{1,0:T(8,128)(2,1)S(1)}, bf16[1792,7168]{1,0:T(8,128)(2,1)}, u32[]{:S(2)}) %copy-start.6) | copy-done | bytes 25690136
  44.8 5.8 %matmul_keep.11 = (bf16[384,1024]{1,0:T(8,128)(2,1)}, bf16[384,1024]{1,0:T(8,128)(2,1)S(1)}, f32[8,128]{1,0:T(8,128)S(1)}) custom-call(s32[2]{0:T(128)S(1)} %pad_add_fusion.here_ref.after_ref, bf16[2,768,1792]{2,1,0:T(8,128)(2,1)S(1)} %bitcast.29, bf16[1792,7168]{1,0:T(8,128)(2,1)S(1)} %copy-done.6, bf16[768,1024]{1,0:T(8,128)(2,1)S(1)} %collective-permute-done.2.recv_ref, ...), custom_call_target="tpu_custom_call" | custom-call | flops 24999999488 | bytes 1024 | tf_op jit(solution)/shard_map/matmul_keep/pallas_call | solution.py:314
  65.1 5.2 %matmul_keep.12 = (bf16[384,1024]{1,0:T(8,128)(2,1)S(1)}, bf16[384,1024]{1,0:T(8,128)(2,1)S(1)}, f32[8,128]{1,0:T(8,128)S(1)}) custom-call(s32[2]{0:T(128)S(1)} %pad_add_fusion.here_ref.after_ref, bf16[2,768,1792]{2,1,0:T(8,128)(2,1)S(1)} %bitcast.31, bf16[1792,7168]{1,0:T(8,128)(2,1)S(1)} %copy-done.6, ...), custom_call_target="tpu_custom_call" | custom-call | flops 24999999488 | bytes 1024 | tf_op jit(solution)/shard_map/matmul_keep/pallas_call | solution.py:314
  88.7 6.8 %collective-permute-start.16 = (bf16[4,3,64,512]{3,2,1,0:T(8,128)(2,1)S(1)}, bf16[4,3,64,512]{3,2,1,0:T(8,128)(2,1)S(1)}, u32[]{:S(2)}, u32[]{:S(2)}) collective-permute-start(bf16[4,3,64,512]{3,2,1,0:T(8,128)(2,1)S(1)} %get-tuple-element.209.refs_0_), channel_id=1, source_target_pairs={{0,2},{1,3},{6,4},{7,5},{8,10},{9,11},{14,12},{15,13},{16,18},{17,... | collective-permute-start | bytes 2359304 | tf_op jit(solution)/shard_map/ppermute | solution.py:537
  96.2 5.2 %matmul_keep.13 = (bf16[384,1024]{1,0:T(8,128)(2,1)S(1)}, bf16[384,1024]{1,0:T(8,128)(2,1)S(1)}, f32[8,128]{1,0:T(8,128)S(1)}) custom-call(s32[2]{0:T(128)S(1)} %pad_add_fusion.here_ref.after_ref, bf16[2,768,1792]{2,1,0:T(8,128)(2,1)S(1)} %bitcast.33, bf16[1792,7168]{1,0:T(8,128)(2,1)S(1)} %copy-done.6, ...), custom_call_target="tpu_custom_call" | custom-call | flops 24999999488 | bytes 1024 | tf_op jit(solution)/shard_map/matmul_keep/pallas_call | solution.py:314
  106.2 6.6 %collective-permute-done.16.refs_1_ = bf16[4,3,64,512]{3,2,1,0:T(8,128)(2,1)S(1)} collective-permute-done((bf16[4,3,64,512]{3,2,1,0:T(8,128)(2,1)S(1)}, bf16[4,3,64,512]{3,2,1,0:T(8,128)(2,1)S(1)}, u32[]{:S(2)}, u32[]{:S(2)}) %collective-permute-start.16) | collective-permute-done | bytes 786464 | tf_op jit(solution)/shard_map/ppermute | solution.py:537
  119.6 6.7 %collective-permute-start.17 = (bf16[4,3,64,512]{3,2,1,0:T(8,128)(2,1)S(1)}, bf16[4,3,64,512]{3,2,1,0:T(8,128)(2,1)S(1)}, u32[]{:S(2)}, u32[]{:S(2)}) collective-permute-start(bf16[4,3,64,512]{3,2,1,0:T(8,128)(2,1)S(1)} %get-tuple-element.212.refs_0_), channel_id=1, source_target_pairs={{0,2},{1,3},{6,4},{7,5},{8,10},{9,11},{14,12},{15,13},{16,18},{17,... | collective-permute-start | bytes 2359304 | tf_op jit(solution)/shard_map/ppermute | solution.py:537
  130.3 9.0 %collective-permute-done.20.side_ref = bf16[2,3,64,512]{3,2,1,0:T(8,128)(2,1)S(1)} collective-permute-done((bf16[2,3,64,512]{3,2,1,0:T(8,128)(2,1)S(1)}, bf16[2,3,64,512]{3,2,1,0:T(8,128)(2,1)S(1)}, u32[]{:S(2)}, u32[]{:S(2)}) %collective-permute-start.20) | collective-permute-done | bytes 393248 | tf_op jit(solution)/shard_map/ppermute | solution.py:532
  162.8 5.2 %matmul_keep.14 = (bf16[384,1024]{1,0:T(8,128)(2,1)S(1)}, bf16[384,1024]{1,0:T(8,128)(2,1)S(1)}, f32[8,128]{1,0:T(8,128)S(1)}) custom-call(s32[2]{0:T(128)S(1)} %pad_add_fusion.here_ref.after_ref, bf16[2,768,1792]{2,1,0:T(8,128)(2,1)S(1)} %bitcast.35, bf16[1792,7168]{1,0:T(8,128)(2,1)S(1)} %copy-done.6, ...), custom_call_target="tpu_custom_call" | custom-call | flops 24999999488 | bytes 1024 | tf_op jit(solution)/shard_map/matmul_keep/pallas_call | solution.py:314
  178.3 5.2 %matmul_keep.15 = (bf16[384,1024]{1,0:T(8,128)(2,1)S(1)}, bf16[384,1024]{1,0:T(8,128)(2,1)S(1)}, f32[8,128]{1,0:T(8,128)S(1)}) custom-call(s32[2]{0:T(128)S(1)} %pad_add_fusion.here_ref.after_ref, bf16[2,768,1792]{2,1,0:T(8,128)(2,1)S(1)} %bitcast.37, bf16[1792,7168]{1,0:T(8,128)(2,1)S(1)} %copy-done.6, ...), custom_call_target="tpu_custom_call" | custom-call | flops 24999999488 | bytes 1024 | tf_op jit(solution)/shard_map/matmul_keep/pallas_call | solution.py:314
  194.5 8.3 %collective-permute-done.32.refs_3_ = bf16[8,3,64,512]{3,2,1,0:T(8,128)(2,1)} collective-permute-done((bf16[8,3,64,512]{3,2,1,0:T(8,128)(2,1)}, bf16[8,3,64,512]{3,2,1,0:T(8,128)(2,1)}, u32[]{:S(2)}, u32[]{:S(2)}) %collective-permute-start.32) | collective-permute-done | bytes 1572896 | tf_op jit(solution)/shard_map/ppermute | solution.py:549
  207.2 5.7 %collective-permute-start.39 = (bf16[4,3,64,512]{3,2,1,0:T(8,128)(2,1)S(1)}, bf16[4,3,64,512]{3,2,1,0:T(8,128)(2,1)S(1)}, u32[]{:S(2)}, u32[]{:S(2)}) collective-permute-start(bf16[4,3,64,512]{3,2,1,0:T(8,128)(2,1)S(1)} %get-tuple-element.263.refs_0_), channel_id=1, source_target_pairs={{0,2},{1,3},{6,4},{7,5},{8,10},{9,11},{14,12},{15,13},{16,18},{17,... | collective-permute-start | bytes 2359304 | tf_op jit(solution)/shard_map/ppermute | solution.py:537
  214.7 10.0 %collective-permute-done.33.refs_4_ = bf16[4,3,64,512]{3,2,1,0:T(8,128)(2,1)S(1)} collective-permute-done((bf16[4,3,64,512]{3,2,1,0:T(8,128)(2,1)S(1)}, bf16[4,3,64,512]{3,2,1,0:T(8,128)(2,1)S(1)}, u32[]{:S(2)}, u32[]{:S(2)}) %collective-permute-start.33) | collective-permute-done | bytes 786464 | tf_op jit(solution)/shard_map/ppermute | solution.py:555
  232.9 5.1 %collective-permute-start.41 = (bf16[4,3,64,512]{3,2,1,0:T(8,128)(2,1)S(1)}, bf16[4,3,64,512]{3,2,1,0:T(8,128)(2,1)S(1)}, u32[]{:S(2)}, u32[]{:S(2)}) collective-permute-start(bf16[4,3,64,512]{3,2,1,0:T(8,128)(2,1)S(1)} %get-tuple-element.270.refs_0_), channel_id=1, source_target_pairs={{0,2},{1,3},{6,4},{7,5},{8,10},{9,11},{14,12},{15,13},{16,18},{17,... | collective-permute-start | bytes 2359304 | tf_op jit(solution)/shard_map/ppermute | solution.py:537
  248.2 8.9 %collective-permute-done.42.recv_ref = bf16[384,512]{1,0:T(8,128)(2,1)S(1)} collective-permute-done((bf16[384,512]{1,0:T(8,128)(2,1)S(1)}, bf16[384,512]{1,0:T(8,128)(2,1)S(1)}, u32[]{:S(2)}, u32[]{:S(2)}) %collective-permute-start.42) | collective-permute-done | bytes 393248 | tf_op jit(solution)/shard_map/ppermute | solution.py:525
  261.8 6.5 %collective-permute-done.40.refs_4_ = bf16[4,3,64,512]{3,2,1,0:T(8,128)(2,1)S(1)} collective-permute-done((bf16[4,3,64,512]{3,2,1,0:T(8,128)(2,1)S(1)}, bf16[4,3,64,512]{3,2,1,0:T(8,128)(2,1)S(1)}, u32[]{:S(2)}, u32[]{:S(2)}) %collective-permute-start.40) | collective-permute-done | bytes 786464 | tf_op jit(solution)/shard_map/ppermute | solution.py:555
  274.5 6.7 %collective-permute-start.47 = (bf16[4,3,64,256]{3,2,1,0:T(8,128)(2,1)S(1)}, bf16[4,3,64,256]{3,2,1,0:T(8,128)(2,1)S(1)}, u32[]{:S(2)}, u32[]{:S(2)}) collective-permute-start(bf16[4,3,64,256]{3,2,1,0:T(8,128)(2,1)S(1)} %get-tuple-element.287.refs_0_), channel_id=1, source_target_pairs={{0,2},{1,3},{6,4},{7,5},{8,10},{9,11},{14,12},{15,13},{16,18},{17,... | collective-permute-start | bytes 1179656 | tf_op jit(solution)/shard_map/ppermute | solution.py:537
  300.6 12.8 %collective-permute-done.51.refs_4_ = bf16[4,3,64,512]{3,2,1,0:T(8,128)(2,1)S(1)} collective-permute-done((bf16[4,3,64,512]{3,2,1,0:T(8,128)(2,1)S(1)}, bf16[4,3,64,512]{3,2,1,0:T(8,128)(2,1)S(1)}, u32[]{:S(2)}, u32[]{:S(2)}) %collective-permute-start.51) | collective-permute-done | bytes 786464 | tf_op jit(solution)/shard_map/ppermute | solution.py:555
  317.6 10.5 %collective-permute-start.52 = (bf16[4,3,64,256]{3,2,1,0:T(8,128)(2,1)S(1)}, bf16[4,3,64,256]{3,2,1,0:T(8,128)(2,1)S(1)}, u32[]{:S(2)}, u32[]{:S(2)}) collective-permute-start(bf16[4,3,64,256]{3,2,1,0:T(8,128)(2,1)S(1)} %get-tuple-element.300.refs_0_), channel_id=1, source_target_pairs={{0,2},{1,3},{6,4},{7,5},{8,10},{9,11},{14,12},{15,13},{16,18},{17,... | collective-permute-start | bytes 1179656 | tf_op jit(solution)/shard_map/ppermute | solution.py:537
  337.0 9.7 %collective-permute-done.55.refs_4_ = bf16[4,3,64,512]{3,2,1,0:T(8,128)(2,1)S(1)} collective-permute-done((bf16[4,3,64,512]{3,2,1,0:T(8,128)(2,1)S(1)}, bf16[4,3,64,512]{3,2,1,0:T(8,128)(2,1)S(1)}, u32[]{:S(2)}, u32[]{:S(2)}) %collective-permute-start.55) | collective-permute-done | bytes 786464 | tf_op jit(solution)/shard_map/ppermute | solution.py:555
  351.7 15.7 %collective-permute-done.58.refs_3_ = bf16[8,3,64,512]{3,2,1,0:T(8,128)(2,1)S(1)} collective-permute-done((bf16[8,3,64,512]{3,2,1,0:T(8,128)(2,1)S(1)}, bf16[8,3,64,512]{3,2,1,0:T(8,128)(2,1)S(1)}, u32[]{:S(2)}, u32[]{:S(2)}) %collective-permute-start.58) | collective-permute-done | bytes 1572896 | tf_op jit(solution)/shard_map/ppermute | solution.py:549
  368.8 15.4 %collective-permute-done.60.refs_3_ = bf16[8,3,64,256]{3,2,1,0:T(8,128)(2,1)S(1)} collective-permute-done((bf16[8,3,64,256]{3,2,1,0:T(8,128)(2,1)S(1)}, bf16[8,3,64,256]{3,2,1,0:T(8,128)(2,1)S(1)}, u32[]{:S(2)}, u32[]{:S(2)}) %collective-permute-start.60) | collective-permute-done | bytes 786464 | tf_op jit(solution)/shard_map/ppermute | solution.py:549
  388.4 7.7 %collective-permute-done.57.refs_3_ = bf16[8,3,64,256]{3,2,1,0:T(8,128)(2,1)S(1)} collective-permute-done((bf16[8,3,64,256]{3,2,1,0:T(8,128)(2,1)S(1)}, bf16[8,3,64,256]{3,2,1,0:T(8,128)(2,1)S(1)}, u32[]{:S(2)}, u32[]{:S(2)}) %collective-permute-start.57) | collective-permute-done | bytes 786464 | tf_op jit(solution)/shard_map/ppermute | solution.py:549
  (213 shorter events, 210.3 us)
Async XLA Ops:
  79.1 22.4 %collective-permute-start.10 = (bf16[8,3,64,256]{3,2,1,0:T(8,128)(2,1)S(1)}, bf16[8,3,64,256]{3,2,1,0:T(8,128)(2,1)S(1)}, u32[]{:S(2)}, u32[]{:S(2)}) collective-permute-start(bf16[8,3,64,256]{3,2,1,0:T(8,128)(2,1)S(1)} %get-tuple-element.193), channel_id=1, source_target_pairs={{2,4},{3,5},{4,2},{5,3},{10,12},{11,13},{12,10},{13,11},{18,20},{1... | collective-permute-start | bytes 2359304 | tf_op jit(solution)/shard_map/ppermute | solution.py:543
  80.0 22.3 %collective-permute-start.7 = (bf16[384,1024]{1,0:T(8,128)(2,1)S(1)}, bf16[384,1024]{1,0:T(8,128)(2,1)S(1)}, u32[]{:S(2)}, u32[]{:S(2)}) collective-permute-start(bf16[384,1024]{1,0:T(8,128)(2,1)S(1)} %get-tuple-element.187), channel_id=1, source_target_pairs={{0,16},{8,24},{16,0},{24,8},{1,17},{9,25},{17,1},{25,9},{2,18},{10... | collective-permute-start | bytes 2359304 | tf_op jit(solution)/shard_map/ppermute | solution.py:525
  88.7 24.1 %collective-permute-start.16 = (bf16[4,3,64,512]{3,2,1,0:T(8,128)(2,1)S(1)}, bf16[4,3,64,512]{3,2,1,0:T(8,128)(2,1)S(1)}, u32[]{:S(2)}, u32[]{:S(2)}) collective-permute-start(bf16[4,3,64,512]{3,2,1,0:T(8,128)(2,1)S(1)} %get-tuple-element.209.refs_0_), channel_id=1, source_target_pairs={{0,2},{1,3},{6,4},{7,5},{8,10},{9,11},{14,12},{15,13},{16,18},{17,... | collective-permute-start | bytes 2359304 | tf_op jit(solution)/shard_map/ppermute | solution.py:537
  103.6 24.1 %collective-permute-start.21 = (bf16[8,3,64,256]{3,2,1,0:T(8,128)(2,1)S(1)}, bf16[8,3,64,256]{3,2,1,0:T(8,128)(2,1)S(1)}, u32[]{:S(2)}, u32[]{:S(2)}) collective-permute-start(bf16[8,3,64,256]{3,2,1,0:T(8,128)(2,1)S(1)} %get-tuple-element.220), channel_id=1, source_target_pairs={{4,6},{5,7},{2,0},{3,1},{12,14},{13,15},{10,8},{11,9},{20,22},{21,... | collective-permute-start | bytes 2359304 | tf_op jit(solution)/shard_map/ppermute | solution.py:549
  114.7 42.6 %collective-permute-start.27 = (bf16[8,3,64,512]{3,2,1,0:T(8,128)(2,1)}, bf16[8,3,64,512]{3,2,1,0:T(8,128)(2,1)}, u32[]{:S(2)}, u32[]{:S(2)}) collective-permute-start(bf16[8,3,64,512]{3,2,1,0:T(8,128)(2,1)} %get-tuple-element.232), channel_id=1, source_target_pairs={{2,4},{3,5},{4,2},{5,3},{10,12},{11,13},{12,10},{13,11},{18,20},{1... | collective-permute-start | bytes 4718600 | tf_op jit(solution)/shard_map/ppermute | solution.py:543
  118.3 27.9 %collective-permute-start.24 = (bf16[8,3,64,256]{3,2,1,0:T(8,128)(2,1)S(1)}, bf16[8,3,64,256]{3,2,1,0:T(8,128)(2,1)S(1)}, u32[]{:S(2)}, u32[]{:S(2)}) collective-permute-start(bf16[8,3,64,256]{3,2,1,0:T(8,128)(2,1)S(1)} %get-tuple-element.226), channel_id=1, source_target_pairs={{4,6},{5,7},{2,0},{3,1},{12,14},{13,15},{10,8},{11,9},{20,22},{21,... | collective-permute-start | bytes 2359304 | tf_op jit(solution)/shard_map/ppermute | solution.py:549
  119.6 24.6 %collective-permute-start.17 = (bf16[4,3,64,512]{3,2,1,0:T(8,128)(2,1)S(1)}, bf16[4,3,64,512]{3,2,1,0:T(8,128)(2,1)S(1)}, u32[]{:S(2)}, u32[]{:S(2)}) collective-permute-start(bf16[4,3,64,512]{3,2,1,0:T(8,128)(2,1)S(1)} %get-tuple-element.212.refs_0_), channel_id=1, source_target_pairs={{0,2},{1,3},{6,4},{7,5},{8,10},{9,11},{14,12},{15,13},{16,18},{17,... | collective-permute-start | bytes 2359304 | tf_op jit(solution)/shard_map/ppermute | solution.py:537
  128.5 21.6 %collective-permute-start.23 = (bf16[4,3,64,256]{3,2,1,0:T(8,128)(2,1)S(1)}, bf16[4,3,64,256]{3,2,1,0:T(8,128)(2,1)S(1)}, u32[]{:S(2)}, u32[]{:S(2)}) collective-permute-start(bf16[4,3,64,256]{3,2,1,0:T(8,128)(2,1)S(1)} %get-tuple-element.225), channel_id=1, source_target_pairs={{0,1},{1,0},{2,3},{3,2},{4,5},{5,4},{6,7},{7,6},{8,9},{9,8},{10,11... | collective-permute-start | bytes 1179656 | tf_op jit(solution)/shard_map/ppermute | solution.py:555
  140.6 34.0 %collective-permute-start.30 = (bf16[4,3,64,512]{3,2,1,0:T(8,128)(2,1)}, bf16[4,3,64,512]{3,2,1,0:T(8,128)(2,1)}, u32[]{:S(2)}, u32[]{:S(2)}) collective-permute-start(bf16[4,3,64,512]{3,2,1,0:T(8,128)(2,1)} %get-tuple-element.241.refs_0_), channel_id=1, source_target_pairs={{0,2},{1,3},{6,4},{7,5},{8,10},{9,11},{14,12},{15,13},{16,18},{17,... | collective-permute-start | bytes 2359304 | tf_op jit(solution)/shard_map/ppermute | solution.py:537
  148.3 44.3 %collective-permute-start.22 = (bf16[8,3,64,512]{3,2,1,0:T(8,128)(2,1)}, bf16[8,3,64,512]{3,2,1,0:T(8,128)(2,1)}, u32[]{:S(2)}, u32[]{:S(2)}) collective-permute-start(bf16[8,3,64,512]{3,2,1,0:T(8,128)(2,1)} %get-tuple-element.224), channel_id=1, source_target_pairs={{2,4},{3,5},{4,2},{5,3},{10,12},{11,13},{12,10},{13,11},{18,20},{1... | collective-permute-start | bytes 4718600 | tf_op jit(solution)/shard_map/ppermute | solution.py:543
  159.2 43.6 %collective-permute-start.32 = (bf16[8,3,64,512]{3,2,1,0:T(8,128)(2,1)}, bf16[8,3,64,512]{3,2,1,0:T(8,128)(2,1)}, u32[]{:S(2)}, u32[]{:S(2)}) collective-permute-start(bf16[8,3,64,512]{3,2,1,0:T(8,128)(2,1)} %get-tuple-element.247), channel_id=1, source_target_pairs={{4,6},{5,7},{2,0},{3,1},{12,14},{13,15},{10,8},{11,9},{20,22},{21,... | collective-permute-start | bytes 4718600 | tf_op jit(solution)/shard_map/ppermute | solution.py:549
  176.5 61.5 %collective-permute-start.37 = (bf16[8,3,64,512]{3,2,1,0:T(8,128)(2,1)}, bf16[8,3,64,512]{3,2,1,0:T(8,128)(2,1)}, u32[]{:S(2)}, u32[]{:S(2)}) collective-permute-start(bf16[8,3,64,512]{3,2,1,0:T(8,128)(2,1)} %get-tuple-element.260), channel_id=1, source_target_pairs={{2,4},{3,5},{4,2},{5,3},{10,12},{11,13},{12,10},{13,11},{18,20},{1... | collective-permute-start | bytes 4718600 | tf_op jit(solution)/shard_map/ppermute | solution.py:543
  190.8 22.1 %collective-permute-start.34 = (bf16[384,1024]{1,0:T(8,128)(2,1)S(1)}, bf16[384,1024]{1,0:T(8,128)(2,1)S(1)}, u32[]{:S(2)}, u32[]{:S(2)}) collective-permute-start(bf16[384,1024]{1,0:T(8,128)(2,1)S(1)} %get-tuple-element.251), channel_id=1, source_target_pairs={{0,16},{8,24},{16,0},{24,8},{1,17},{9,25},{17,1},{25,9},{2,18},{10... | collective-permute-start | bytes 2359304 | tf_op jit(solution)/shard_map/ppermute | solution.py:525
  205.5 40.8 %collective-permute-start.31 = (bf16[8,3,64,512]{3,2,1,0:T(8,128)(2,1)}, bf16[8,3,64,512]{3,2,1,0:T(8,128)(2,1)}, u32[]{:S(2)}, u32[]{:S(2)}) collective-permute-start(bf16[8,3,64,512]{3,2,1,0:T(8,128)(2,1)} %get-tuple-element.246), channel_id=1, source_target_pairs={{4,6},{5,7},{2,0},{3,1},{12,14},{13,15},{10,8},{11,9},{20,22},{21,... | collective-permute-start | bytes 4718600 | tf_op jit(solution)/shard_map/ppermute | solution.py:549
  207.2 23.2 %collective-permute-start.39 = (bf16[4,3,64,512]{3,2,1,0:T(8,128)(2,1)S(1)}, bf16[4,3,64,512]{3,2,1,0:T(8,128)(2,1)S(1)}, u32[]{:S(2)}, u32[]{:S(2)}) collective-permute-start(bf16[4,3,64,512]{3,2,1,0:T(8,128)(2,1)S(1)} %get-tuple-element.263.refs_0_), channel_id=1, source_target_pairs={{0,2},{1,3},{6,4},{7,5},{8,10},{9,11},{14,12},{15,13},{16,18},{17,... | collective-permute-start | bytes 2359304 | tf_op jit(solution)/shard_map/ppermute | solution.py:537
  232.9 25.1 %collective-permute-start.41 = (bf16[4,3,64,512]{3,2,1,0:T(8,128)(2,1)S(1)}, bf16[4,3,64,512]{3,2,1,0:T(8,128)(2,1)S(1)}, u32[]{:S(2)}, u32[]{:S(2)}) collective-permute-start(bf16[4,3,64,512]{3,2,1,0:T(8,128)(2,1)S(1)} %get-tuple-element.270.refs_0_), channel_id=1, source_target_pairs={{0,2},{1,3},{6,4},{7,5},{8,10},{9,11},{14,12},{15,13},{16,18},{17,... | collective-permute-start | bytes 2359304 | tf_op jit(solution)/shard_map/ppermute | solution.py:537
  239.8 48.4 %collective-permute-start.48 = (bf16[8,3,64,512]{3,2,1,0:T(8,128)(2,1)}, bf16[8,3,64,512]{3,2,1,0:T(8,128)(2,1)}, u32[]{:S(2)}, u32[]{:S(2)}) collective-permute-start(bf16[8,3,64,512]{3,2,1,0:T(8,128)(2,1)} %get-tuple-element.288), channel_id=1, source_target_pairs={{4,6},{5,7},{2,0},{3,1},{12,14},{13,15},{10,8},{11,9},{20,22},{21,... | collective-permute-start | bytes 4718600 | tf_op jit(solution)/shard_map/ppermute | solution.py:549
  241.1 40.1 %collective-permute-start.44 = (bf16[8,3,64,512]{3,2,1,0:T(8,128)(2,1)}, bf16[8,3,64,512]{3,2,1,0:T(8,128)(2,1)}, u32[]{:S(2)}, u32[]{:S(2)}) collective-permute-start(bf16[8,3,64,512]{3,2,1,0:T(8,128)(2,1)} %get-tuple-element.279), channel_id=1, source_target_pairs={{2,4},{3,5},{4,2},{5,3},{10,12},{11,13},{12,10},{13,11},{18,20},{1... | collective-permute-start | bytes 4718600 | tf_op jit(solution)/shard_map/ppermute | solution.py:543
  260.0 56.4 %collective-permute-start.50 = (bf16[8,3,64,512]{3,2,1,0:T(8,128)(2,1)}, bf16[8,3,64,512]{3,2,1,0:T(8,128)(2,1)}, u32[]{:S(2)}, u32[]{:S(2)}) collective-permute-start(bf16[8,3,64,512]{3,2,1,0:T(8,128)(2,1)} %get-tuple-element.294), channel_id=1, source_target_pairs={{2,4},{3,5},{4,2},{5,3},{10,12},{11,13},{12,10},{13,11},{18,20},{1... | collective-permute-start | bytes 4718600 | tf_op jit(solution)/shard_map/ppermute | solution.py:543
  283.2 46.3 %collective-permute-start.53 = (bf16[8,3,64,512]{3,2,1,0:T(8,128)(2,1)}, bf16[8,3,64,512]{3,2,1,0:T(8,128)(2,1)}, u32[]{:S(2)}, u32[]{:S(2)}) collective-permute-start(bf16[8,3,64,512]{3,2,1,0:T(8,128)(2,1)} %get-tuple-element.301), channel_id=1, source_target_pairs={{4,6},{5,7},{2,0},{3,1},{12,14},{13,15},{10,8},{11,9},{20,22},{21,... | collective-permute-start | bytes 4718600 | tf_op jit(solution)/shard_map/ppermute | solution.py:549
  291.5 42.7 %collective-permute-start.56 = (bf16[8,3,64,256]{3,2,1,0:T(8,128)(2,1)}, bf16[8,3,64,256]{3,2,1,0:T(8,128)(2,1)}, u32[]{:S(2)}, u32[]{:S(2)}) collective-permute-start(bf16[8,3,64,256]{3,2,1,0:T(8,128)(2,1)} %get-tuple-element.306), channel_id=1, source_target_pairs={{2,4},{3,5},{4,2},{5,3},{10,12},{11,13},{12,10},{13,11},{18,20},{1... | collective-permute-start | bytes 2359304 | tf_op jit(solution)/shard_map/ppermute | solution.py:543
  328.2 39.2 %collective-permute-start.58 = (bf16[8,3,64,512]{3,2,1,0:T(8,128)(2,1)S(1)}, bf16[8,3,64,512]{3,2,1,0:T(8,128)(2,1)S(1)}, u32[]{:S(2)}, u32[]{:S(2)}) collective-permute-start(bf16[8,3,64,512]{3,2,1,0:T(8,128)(2,1)S(1)} %get-tuple-element.312), channel_id=1, source_target_pairs={{4,6},{5,7},{2,0},{3,1},{12,14},{13,15},{10,8},{11,9},{20,22},{21,... | collective-permute-start | bytes 4718600 | tf_op jit(solution)/shard_map/ppermute | solution.py:549
  334.9 49.3 %collective-permute-start.60 = (bf16[8,3,64,256]{3,2,1,0:T(8,128)(2,1)S(1)}, bf16[8,3,64,256]{3,2,1,0:T(8,128)(2,1)S(1)}, u32[]{:S(2)}, u32[]{:S(2)}) collective-permute-start(bf16[8,3,64,256]{3,2,1,0:T(8,128)(2,1)S(1)} %get-tuple-element.315), channel_id=1, source_target_pairs={{4,6},{5,7},{2,0},{3,1},{12,14},{13,15},{10,8},{11,9},{20,22},{21,... | collective-permute-start | bytes 2359304 | tf_op jit(solution)/shard_map/ppermute | solution.py:549
  350.4 45.7 %collective-permute-start.57 = (bf16[8,3,64,256]{3,2,1,0:T(8,128)(2,1)S(1)}, bf16[8,3,64,256]{3,2,1,0:T(8,128)(2,1)S(1)}, u32[]{:S(2)}, u32[]{:S(2)}) collective-permute-start(bf16[8,3,64,256]{3,2,1,0:T(8,128)(2,1)S(1)} %get-tuple-element.311), channel_id=1, source_target_pairs={{4,6},{5,7},{2,0},{3,1},{12,14},{13,15},{10,8},{11,9},{20,22},{21,... | collective-permute-start | bytes 2359304 | tf_op jit(solution)/shard_map/ppermute | solution.py:549
  (57 other events, 608.1 us)

commit v3 on v2

--- a/solution.py
+++ b/solution.py
@@ -8,7 +8,7 @@
 from jax.sharding import PartitionSpec as P
 
 CHUNK_TILES = (1, 1, 2, 2, 2, 2, 2, 1, 1)
-MATMUL_VMEM = 16 * 2**20
+MATMUL_VMEM = 36 * 2**20
 MOVE_VMEM = 8 * 2**20
 COST = pl.CostEstimate(flops=25000000000, bytes_accessed=2**10, transcendentals=0)
 ORDER = (

time: 407 us -> 403 us (level)
  Pallas kernels: 149 us -> 172 us
  local copies, waits for them, and re-layouts: 21.7 us -> 5.16 us
  waiting for transfers between devices: 130 us -> 115 us
    unnamed x36 -> x40, local copies, waits for them, and re-layouts: 21.7 us -> 5.16 us
    pallas_call x9, Pallas kernels: 34.9 us -> 43.4 us  [matmul_send(): pl.pallas_call(functools.partial(send_kernel, column=column), out_shape=(...]
    pallas_call x9, Pallas kernels: 38.2 us -> 46.4 us  [matmul_keep(): pl.pallas_call(functools.partial(keep_kernel, column=column), out_shape=(...]
    ppermute x9, waiting for transfers between devices: 47.1 us -> 42.2 us  [send_outward(): outer[i] = lax.ppermute(out, 'ep', outward)]
    pallas_call x9, Pallas kernels: 23.6 us -> 28.4 us  [place(): pl.pallas_call(functools.partial(place_kernel, bases=bases, column=column...]
    ppermute x9, starting transfers between devices: 7.42 us -> 12.2 us  [send_partner(): partner[i] = lax.ppermute(out, 'ep', along_y)]
  transfers between devices with their start and end apart: 63 -> 63, of which waited for: 21 -> 17; matrix products, arithmetic and copies ran while one was open for 0% -> 0% of each run, Pallas kernels for 34% -> 40%
where the time goes in v3:
time: 403 us; the launch traced here: 400 us
  Pallas kernels  172 us (43%)
  waiting for transfers between devices  115 us (29%)
  starting transfers between devices  107 us (27%)
  local copies, waits for them, and re-layouts  5.16 us (1%)
    ppermute x9, starting transfers between devices, send_inward(): far[i] = lax.ppermute(near[i], 'ep', inward)  48.8 us
    pallas_call x9, Pallas kernels, matmul_keep(): pl.pallas_call(functools.partial(keep_kernel, column=column), out_shape=(...  46.4 us
    pallas_call x9, Pallas kernels, matmul_send(): pl.pallas_call(functools.partial(send_kernel, column=column), out_shape=(...  43.4 us
    ppermute x9, waiting for transfers between devices, send_outward(): outer[i] = lax.ppermute(out, 'ep', outward)  42.2 us
    ppermute x9, waiting for transfers between devices, send_partner(): partner[i] = lax.ppermute(out, 'ep', along_y)  40.7 us
    pallas_call x27, Pallas kernels, pick(): pl.pallas_call(functools.partial(pick_kernel, first=first, bases=bases),...  37.1 us
    pallas_call x9, Pallas kernels, place(): pl.pallas_call(functools.partial(place_kernel, bases=bases, column=column...  28.4 us
    ppermute x9, waiting for transfers between devices, keep_terms(): x_recv[i] = lax.ppermute(away, 'hid', along_x)  14.6 us
  transfers between devices with their start and end apart: 63, of which 17 were waited for; matrix products, arithmetic and copies ran while one was open for 0% of the time, Pallas kernels for 40%

profile of v3, /device:TPU:0, one launch (start us, length us, event | category | flops | bytes accessed | tf_op | source)
XLA Modules:
  0.0 400.2 jit_solution(8055809303007713063)
XLA Ops:
  22.6 5.8 %matmul_send.11 = (bf16[768,1024]{1,0:T(8,128)(2,1)S(1)}, f32[8,128]{1,0:T(8,128)S(1)}) custom-call(s32[2]{0:T(128)S(1)} %pad_add_fusion.here_ref.after_ref, bf16[2,768,1792]{2,1,0:T(8,128)(2,1)S(1)} %bitcast.27, bf16[1792,7168]{1,0:T(8,128)(2,1)} %rot_ref.35, f32[8,128]{1,0:T(8,128)S(1)} %get-tuple-element.171.after_ref), custom_call_target="tpu_custom_call" | custom-call | flops 24999999488 | bytes 1024 | tf_op jit(solution)/shard_map/matmul_send/pallas_call | solution.py:293
  32.8 6.7 %matmul_keep.11 = (bf16[384,1024]{1,0:T(8,128)(2,1)}, bf16[384,1024]{1,0:T(8,128)(2,1)S(1)}, f32[8,128]{1,0:T(8,128)S(1)}) custom-call(s32[2]{0:T(128)S(1)} %pad_add_fusion.here_ref.after_ref, bf16[2,768,1792]{2,1,0:T(8,128)(2,1)S(1)} %bitcast.29, bf16[1792,7168]{1,0:T(8,128)(2,1)} %rot_ref.35, bf16[768,1024]{1,0:T(8,128)(2,1)S(1)} %collective-permute-done.2.recv_ref, ...), custom_call_target="tpu_custom_call" | custom-call | flops 24999999488 | bytes 1024 | tf_op jit(solution)/shard_map/matmul_keep/pallas_call | solution.py:314
  43.9 5.8 %matmul_send.12 = (bf16[768,1024]{1,0:T(8,128)(2,1)S(1)}, f32[8,128]{1,0:T(8,128)S(1)}) custom-call(s32[2]{0:T(128)S(1)} %pad_add_fusion.here_ref.after_ref, bf16[2,768,1792]{2,1,0:T(8,128)(2,1)S(1)} %bitcast.30, bf16[1792,7168]{1,0:T(8,128)(2,1)} %rot_ref.35, f32[8,128]{1,0:T(8,128)S(1)} %get-tuple-element.177.after_ref), custom_call_target="tpu_custom_call" | custom-call | flops 24999999488 | bytes 1024 | tf_op jit(solution)/shard_map/matmul_send/pallas_call | solution.py:293
  55.0 6.2 %matmul_keep.12 = (bf16[384,1024]{1,0:T(8,128)(2,1)S(1)}, bf16[384,1024]{1,0:T(8,128)(2,1)S(1)}, f32[8,128]{1,0:T(8,128)S(1)}) custom-call(s32[2]{0:T(128)S(1)} %pad_add_fusion.here_ref.after_ref, bf16[2,768,1792]{2,1,0:T(8,128)(2,1)S(1)} %bitcast.31, bf16[1792,7168]{1,0:T(8,128)(2,1)} %rot_ref.35, bf16[768,1024]{1,0:T(8,128)(2,1)S(1)} %collective-permute-done.4.recv_ref, ...), custom_call_target="tpu_custom_call" | custom-call | flops 24999999488 | bytes 1024 | tf_op jit(solution)/shard_map/matmul_keep/pallas_call | solution.py:314
  70.9 5.8 %matmul_send.13 = (bf16[768,1024]{1,0:T(8,128)(2,1)S(1)}, f32[8,128]{1,0:T(8,128)S(1)}) custom-call(s32[2]{0:T(128)S(1)} %pad_add_fusion.here_ref.after_ref, bf16[2,768,1792]{2,1,0:T(8,128)(2,1)S(1)} %bitcast.32, bf16[1792,7168]{1,0:T(8,128)(2,1)} %rot_ref.35, f32[8,128]{1,0:T(8,128)S(1)} %get-tuple-element.197.after_ref), custom_call_target="tpu_custom_call" | custom-call | flops 24999999488 | bytes 1024 | tf_op jit(solution)/shard_map/matmul_send/pallas_call | solution.py:293
  79.4 6.0 %collective-permute-start.16 = (bf16[4,3,64,512]{3,2,1,0:T(8,128)(2,1)S(1)}, bf16[4,3,64,512]{3,2,1,0:T(8,128)(2,1)S(1)}, u32[]{:S(2)}, u32[]{:S(2)}) collective-permute-start(bf16[4,3,64,512]{3,2,1,0:T(8,128)(2,1)S(1)} %get-tuple-element.209.refs_0_), channel_id=1, source_target_pairs={{0,2},{1,3},{6,4},{7,5},{8,10},{9,11},{14,12},{15,13},{16,18},{17,... | collective-permute-start | bytes 2359304 | tf_op jit(solution)/shard_map/ppermute | solution.py:537
  86.1 6.1 %matmul_keep.13 = (bf16[384,1024]{1,0:T(8,128)(2,1)S(1)}, bf16[384,1024]{1,0:T(8,128)(2,1)S(1)}, f32[8,128]{1,0:T(8,128)S(1)}) custom-call(s32[2]{0:T(128)S(1)} %pad_add_fusion.here_ref.after_ref, bf16[2,768,1792]{2,1,0:T(8,128)(2,1)S(1)} %bitcast.33, bf16[1792,7168]{1,0:T(8,128)(2,1)} %rot_ref.35, bf16[768,1024]{1,0:T(8,128)(2,1)S(1)} %collective-permute-done.12.recv_ref, ...), custom_call_target="tpu_custom_call" | custom-call | flops 24999999488 | bytes 1024 | tf_op jit(solution)/shard_map/matmul_keep/pallas_call | solution.py:314
  109.9 6.4 %collective-permute-start.17 = (bf16[4,3,64,512]{3,2,1,0:T(8,128)(2,1)S(1)}, bf16[4,3,64,512]{3,2,1,0:T(8,128)(2,1)S(1)}, u32[]{:S(2)}, u32[]{:S(2)}) collective-permute-start(bf16[4,3,64,512]{3,2,1,0:T(8,128)(2,1)S(1)} %get-tuple-element.212.refs_0_), channel_id=1, source_target_pairs={{0,2},{1,3},{6,4},{7,5},{8,10},{9,11},{14,12},{15,13},{16,18},{17,... | collective-permute-start | bytes 2359304 | tf_op jit(solution)/shard_map/ppermute | solution.py:537
  120.5 8.7 %collective-permute-done.20.side_ref = bf16[2,3,64,512]{3,2,1,0:T(8,128)(2,1)S(1)} collective-permute-done((bf16[2,3,64,512]{3,2,1,0:T(8,128)(2,1)S(1)}, bf16[2,3,64,512]{3,2,1,0:T(8,128)(2,1)S(1)}, u32[]{:S(2)}, u32[]{:S(2)}) %collective-permute-start.20) | collective-permute-done | bytes 393248 | tf_op jit(solution)/shard_map/ppermute | solution.py:532
  144.0 5.8 %matmul_send.14 = (bf16[768,1024]{1,0:T(8,128)(2,1)S(1)}, f32[8,128]{1,0:T(8,128)S(1)}) custom-call(s32[2]{0:T(128)S(1)} %pad_add_fusion.here_ref.after_ref, bf16[2,768,1792]{2,1,0:T(8,128)(2,1)S(1)} %bitcast.34, bf16[1792,7168]{1,0:T(8,128)(2,1)} %rot_ref.35, f32[8,128]{1,0:T(8,128)S(1)} %get-tuple-element.229.after_ref), custom_call_target="tpu_custom_call" | custom-call | flops 24999999488 | bytes 1024 | tf_op jit(solution)/shard_map/matmul_send/pallas_call | solution.py:293
  155.8 6.1 %matmul_keep.14 = (bf16[384,1024]{1,0:T(8,128)(2,1)S(1)}, bf16[384,1024]{1,0:T(8,128)(2,1)S(1)}, f32[8,128]{1,0:T(8,128)S(1)}) custom-call(s32[2]{0:T(128)S(1)} %pad_add_fusion.here_ref.after_ref, bf16[2,768,1792]{2,1,0:T(8,128)(2,1)S(1)} %bitcast.35, bf16[1792,7168]{1,0:T(8,128)(2,1)} %rot_ref.35, bf16[768,1024]{1,0:T(8,128)(2,1)S(1)} %collective-permute-done.25.recv_ref, ...), custom_call_target="tpu_custom_call" | custom-call | flops 24999999488 | bytes 1024 | tf_op jit(solution)/shard_map/matmul_keep/pallas_call | solution.py:314
  163.5 5.8 %matmul_send.15 = (bf16[768,1024]{1,0:T(8,128)(2,1)S(1)}, f32[8,128]{1,0:T(8,128)S(1)}) custom-call(s32[2]{0:T(128)S(1)} %pad_add_fusion.here_ref.after_ref, bf16[2,768,1792]{2,1,0:T(8,128)(2,1)S(1)} %bitcast.36, bf16[1792,7168]{1,0:T(8,128)(2,1)} %rot_ref.35, f32[8,128]{1,0:T(8,128)S(1)} %get-tuple-element.239.after_ref), custom_call_target="tpu_custom_call" | custom-call | flops 24999999488 | bytes 1024 | tf_op jit(solution)/shard_map/matmul_send/pallas_call | solution.py:293
  173.3 6.1 %matmul_keep.15 = (bf16[384,1024]{1,0:T(8,128)(2,1)S(1)}, bf16[384,1024]{1,0:T(8,128)(2,1)S(1)}, f32[8,128]{1,0:T(8,128)S(1)}) custom-call(s32[2]{0:T(128)S(1)} %pad_add_fusion.here_ref.after_ref, bf16[2,768,1792]{2,1,0:T(8,128)(2,1)S(1)} %bitcast.37, bf16[1792,7168]{1,0:T(8,128)(2,1)} %rot_ref.35, bf16[768,1024]{1,0:T(8,128)(2,1)S(1)} %collective-permute-done.29.recv_ref, ...), custom_call_target="tpu_custom_call" | custom-call | flops 24999999488 | bytes 1024 | tf_op jit(solution)/shard_map/matmul_keep/pallas_call | solution.py:314
  196.7 5.7 %collective-permute-start.39 = (bf16[4,3,64,512]{3,2,1,0:T(8,128)(2,1)S(1)}, bf16[4,3,64,512]{3,2,1,0:T(8,128)(2,1)S(1)}, u32[]{:S(2)}, u32[]{:S(2)}) collective-permute-start(bf16[4,3,64,512]{3,2,1,0:T(8,128)(2,1)S(1)} %get-tuple-element.263.refs_0_), channel_id=1, source_target_pairs={{0,2},{1,3},{6,4},{7,5},{8,10},{9,11},{14,12},{15,13},{16,18},{17,... | collective-permute-start | bytes 2359304 | tf_op jit(solution)/shard_map/ppermute | solution.py:537
  204.7 9.4 %collective-permute-done.33.refs_4_ = bf16[4,3,64,512]{3,2,1,0:T(8,128)(2,1)S(1)} collective-permute-done((bf16[4,3,64,512]{3,2,1,0:T(8,128)(2,1)S(1)}, bf16[4,3,64,512]{3,2,1,0:T(8,128)(2,1)S(1)}, u32[]{:S(2)}, u32[]{:S(2)}) %collective-permute-start.33) | collective-permute-done | bytes 786464 | tf_op jit(solution)/shard_map/ppermute | solution.py:555
  240.7 7.1 %collective-permute-done.42.recv_ref = bf16[384,512]{1,0:T(8,128)(2,1)S(1)} collective-permute-done((bf16[384,512]{1,0:T(8,128)(2,1)S(1)}, bf16[384,512]{1,0:T(8,128)(2,1)S(1)}, u32[]{:S(2)}, u32[]{:S(2)}) %collective-permute-start.42) | collective-permute-done | bytes 393248 | tf_op jit(solution)/shard_map/ppermute | solution.py:525
  252.9 6.2 %collective-permute-done.40.refs_4_ = bf16[4,3,64,512]{3,2,1,0:T(8,128)(2,1)S(1)} collective-permute-done((bf16[4,3,64,512]{3,2,1,0:T(8,128)(2,1)S(1)}, bf16[4,3,64,512]{3,2,1,0:T(8,128)(2,1)S(1)}, u32[]{:S(2)}, u32[]{:S(2)}) %collective-permute-start.40) | collective-permute-done | bytes 786464 | tf_op jit(solution)/shard_map/ppermute | solution.py:555
  266.7 6.6 %collective-permute-start.47 = (bf16[4,3,64,256]{3,2,1,0:T(8,128)(2,1)S(1)}, bf16[4,3,64,256]{3,2,1,0:T(8,128)(2,1)S(1)}, u32[]{:S(2)}, u32[]{:S(2)}) collective-permute-start(bf16[4,3,64,256]{3,2,1,0:T(8,128)(2,1)S(1)} %get-tuple-element.287.refs_0_), channel_id=1, source_target_pairs={{0,2},{1,3},{6,4},{7,5},{8,10},{9,11},{14,12},{15,13},{16,18},{17,... | collective-permute-start | bytes 1179656 | tf_op jit(solution)/shard_map/ppermute | solution.py:537
  294.4 11.6 %collective-permute-done.51.refs_4_ = bf16[4,3,64,512]{3,2,1,0:T(8,128)(2,1)S(1)} collective-permute-done((bf16[4,3,64,512]{3,2,1,0:T(8,128)(2,1)S(1)}, bf16[4,3,64,512]{3,2,1,0:T(8,128)(2,1)S(1)}, u32[]{:S(2)}, u32[]{:S(2)}) %collective-permute-start.51) | collective-permute-done | bytes 786464 | tf_op jit(solution)/shard_map/ppermute | solution.py:555
  310.5 9.6 %collective-permute-start.52 = (bf16[4,3,64,256]{3,2,1,0:T(8,128)(2,1)S(1)}, bf16[4,3,64,256]{3,2,1,0:T(8,128)(2,1)S(1)}, u32[]{:S(2)}, u32[]{:S(2)}) collective-permute-start(bf16[4,3,64,256]{3,2,1,0:T(8,128)(2,1)S(1)} %get-tuple-element.300.refs_0_), channel_id=1, source_target_pairs={{0,2},{1,3},{6,4},{7,5},{8,10},{9,11},{14,12},{15,13},{16,18},{17,... | collective-permute-start | bytes 1179656 | tf_op jit(solution)/shard_map/ppermute | solution.py:537
  329.0 9.4 %collective-permute-done.55.refs_4_ = bf16[4,3,64,512]{3,2,1,0:T(8,128)(2,1)S(1)} collective-permute-done((bf16[4,3,64,512]{3,2,1,0:T(8,128)(2,1)S(1)}, bf16[4,3,64,512]{3,2,1,0:T(8,128)(2,1)S(1)}, u32[]{:S(2)}, u32[]{:S(2)}) %collective-permute-start.55) | collective-permute-done | bytes 786464 | tf_op jit(solution)/shard_map/ppermute | solution.py:555
  344.0 15.4 %collective-permute-done.58.refs_3_ = bf16[8,3,64,512]{3,2,1,0:T(8,128)(2,1)S(1)} collective-permute-done((bf16[8,3,64,512]{3,2,1,0:T(8,128)(2,1)S(1)}, bf16[8,3,64,512]{3,2,1,0:T(8,128)(2,1)S(1)}, u32[]{:S(2)}, u32[]{:S(2)}) %collective-permute-start.58) | collective-permute-done | bytes 1572896 | tf_op jit(solution)/shard_map/ppermute | solution.py:549
  361.6 14.7 %collective-permute-done.60.refs_3_ = bf16[8,3,64,256]{3,2,1,0:T(8,128)(2,1)S(1)} collective-permute-done((bf16[8,3,64,256]{3,2,1,0:T(8,128)(2,1)S(1)}, bf16[8,3,64,256]{3,2,1,0:T(8,128)(2,1)S(1)}, u32[]{:S(2)}, u32[]{:S(2)}) %collective-permute-start.60) | collective-permute-done | bytes 786464 | tf_op jit(solution)/shard_map/ppermute | solution.py:549
  381.9 6.7 %collective-permute-done.57.refs_3_ = bf16[8,3,64,256]{3,2,1,0:T(8,128)(2,1)S(1)} collective-permute-done((bf16[8,3,64,256]{3,2,1,0:T(8,128)(2,1)S(1)}, bf16[8,3,64,256]{3,2,1,0:T(8,128)(2,1)S(1)}, u32[]{:S(2)}, u32[]{:S(2)}) %collective-permute-start.57) | collective-permute-done | bytes 786464 | tf_op jit(solution)/shard_map/ppermute | solution.py:549
  (217 shorter events, 214.9 us)
Async XLA Ops:
  16.0 23.6 %collective-permute-start.1 = (bf16[384,512]{1,0:T(8,128)(2,1)S(1)}, bf16[384,512]{1,0:T(8,128)(2,1)S(1)}, u32[]{:S(2)}, u32[]{:S(2)}) collective-permute-start(bf16[384,512]{1,0:T(8,128)(2,1)S(1)} %get-tuple-element.169), channel_id=1, source_target_pairs={{0,16},{8,24},{16,0},{24,8},{1,17},{9,25},{17,1},{25,9},{2,18},{10... | collective-permute-start | bytes 1179656 | tf_op jit(solution)/shard_map/ppermute | solution.py:525
  42.4 23.0 %collective-permute-start.11 = (bf16[384,1024]{1,0:T(8,128)(2,1)}, bf16[384,1024]{1,0:T(8,128)(2,1)}, u32[]{:S(2)}, u32[]{:S(2)}) collective-permute-start(bf16[384,1024]{1,0:T(8,128)(2,1)} %get-tuple-element.195), channel_id=1, source_target_pairs={{0,16},{8,24},{16,0},{24,8},{1,17},{9,25},{17,1},{25,9},{2,18},{10... | collective-permute-start | bytes 2359304 | tf_op jit(solution)/shard_map/ppermute | solution.py:525
  69.6 22.7 %collective-permute-start.10 = (bf16[8,3,64,256]{3,2,1,0:T(8,128)(2,1)S(1)}, bf16[8,3,64,256]{3,2,1,0:T(8,128)(2,1)S(1)}, u32[]{:S(2)}, u32[]{:S(2)}) collective-permute-start(bf16[8,3,64,256]{3,2,1,0:T(8,128)(2,1)S(1)} %get-tuple-element.193), channel_id=1, source_target_pairs={{2,4},{3,5},{4,2},{5,3},{10,12},{11,13},{12,10},{13,11},{18,20},{1... | collective-permute-start | bytes 2359304 | tf_op jit(solution)/shard_map/ppermute | solution.py:543
  70.3 22.7 %collective-permute-start.7 = (bf16[384,1024]{1,0:T(8,128)(2,1)S(1)}, bf16[384,1024]{1,0:T(8,128)(2,1)S(1)}, u32[]{:S(2)}, u32[]{:S(2)}) collective-permute-start(bf16[384,1024]{1,0:T(8,128)(2,1)S(1)} %get-tuple-element.187), channel_id=1, source_target_pairs={{0,16},{8,24},{16,0},{24,8},{1,17},{9,25},{17,1},{25,9},{2,18},{10... | collective-permute-start | bytes 2359304 | tf_op jit(solution)/shard_map/ppermute | solution.py:525
  79.4 23.4 %collective-permute-start.16 = (bf16[4,3,64,512]{3,2,1,0:T(8,128)(2,1)S(1)}, bf16[4,3,64,512]{3,2,1,0:T(8,128)(2,1)S(1)}, u32[]{:S(2)}, u32[]{:S(2)}) collective-permute-start(bf16[4,3,64,512]{3,2,1,0:T(8,128)(2,1)S(1)} %get-tuple-element.209.refs_0_), channel_id=1, source_target_pairs={{0,2},{1,3},{6,4},{7,5},{8,10},{9,11},{14,12},{15,13},{16,18},{17,... | collective-permute-start | bytes 2359304 | tf_op jit(solution)/shard_map/ppermute | solution.py:537
  94.5 23.3 %collective-permute-start.21 = (bf16[8,3,64,256]{3,2,1,0:T(8,128)(2,1)S(1)}, bf16[8,3,64,256]{3,2,1,0:T(8,128)(2,1)S(1)}, u32[]{:S(2)}, u32[]{:S(2)}) collective-permute-start(bf16[8,3,64,256]{3,2,1,0:T(8,128)(2,1)S(1)} %get-tuple-element.220), channel_id=1, source_target_pairs={{4,6},{5,7},{2,0},{3,1},{12,14},{13,15},{10,8},{11,9},{20,22},{21,... | collective-permute-start | bytes 2359304 | tf_op jit(solution)/shard_map/ppermute | solution.py:549
  104.9 45.0 %collective-permute-start.27 = (bf16[8,3,64,512]{3,2,1,0:T(8,128)(2,1)}, bf16[8,3,64,512]{3,2,1,0:T(8,128)(2,1)}, u32[]{:S(2)}, u32[]{:S(2)}) collective-permute-start(bf16[8,3,64,512]{3,2,1,0:T(8,128)(2,1)} %get-tuple-element.232), channel_id=1, source_target_pairs={{2,4},{3,5},{4,2},{5,3},{10,12},{11,13},{12,10},{13,11},{18,20},{1... | collective-permute-start | bytes 4718600 | tf_op jit(solution)/shard_map/ppermute | solution.py:543
  108.6 28.0 %collective-permute-start.24 = (bf16[8,3,64,256]{3,2,1,0:T(8,128)(2,1)S(1)}, bf16[8,3,64,256]{3,2,1,0:T(8,128)(2,1)S(1)}, u32[]{:S(2)}, u32[]{:S(2)}) collective-permute-start(bf16[8,3,64,256]{3,2,1,0:T(8,128)(2,1)S(1)} %get-tuple-element.226), channel_id=1, source_target_pairs={{4,6},{5,7},{2,0},{3,1},{12,14},{13,15},{10,8},{11,9},{20,22},{21,... | collective-permute-start | bytes 2359304 | tf_op jit(solution)/shard_map/ppermute | solution.py:549
  109.9 24.7 %collective-permute-start.17 = (bf16[4,3,64,512]{3,2,1,0:T(8,128)(2,1)S(1)}, bf16[4,3,64,512]{3,2,1,0:T(8,128)(2,1)S(1)}, u32[]{:S(2)}, u32[]{:S(2)}) collective-permute-start(bf16[4,3,64,512]{3,2,1,0:T(8,128)(2,1)S(1)} %get-tuple-element.212.refs_0_), channel_id=1, source_target_pairs={{0,2},{1,3},{6,4},{7,5},{8,10},{9,11},{14,12},{15,13},{16,18},{17,... | collective-permute-start | bytes 2359304 | tf_op jit(solution)/shard_map/ppermute | solution.py:537
  130.6 39.0 %collective-permute-start.30 = (bf16[4,3,64,512]{3,2,1,0:T(8,128)(2,1)}, bf16[4,3,64,512]{3,2,1,0:T(8,128)(2,1)}, u32[]{:S(2)}, u32[]{:S(2)}) collective-permute-start(bf16[4,3,64,512]{3,2,1,0:T(8,128)(2,1)} %get-tuple-element.241.refs_0_), channel_id=1, source_target_pairs={{0,2},{1,3},{6,4},{7,5},{8,10},{9,11},{14,12},{15,13},{16,18},{17,... | collective-permute-start | bytes 2359304 | tf_op jit(solution)/shard_map/ppermute | solution.py:537
  139.4 44.9 %collective-permute-start.22 = (bf16[8,3,64,512]{3,2,1,0:T(8,128)(2,1)}, bf16[8,3,64,512]{3,2,1,0:T(8,128)(2,1)}, u32[]{:S(2)}, u32[]{:S(2)}) collective-permute-start(bf16[8,3,64,512]{3,2,1,0:T(8,128)(2,1)} %get-tuple-element.224), channel_id=1, source_target_pairs={{2,4},{3,5},{4,2},{5,3},{10,12},{11,13},{12,10},{13,11},{18,20},{1... | collective-permute-start | bytes 4718600 | tf_op jit(solution)/shard_map/ppermute | solution.py:543
  151.7 40.0 %collective-permute-start.32 = (bf16[8,3,64,512]{3,2,1,0:T(8,128)(2,1)}, bf16[8,3,64,512]{3,2,1,0:T(8,128)(2,1)}, u32[]{:S(2)}, u32[]{:S(2)}) collective-permute-start(bf16[8,3,64,512]{3,2,1,0:T(8,128)(2,1)} %get-tuple-element.247), channel_id=1, source_target_pairs={{4,6},{5,7},{2,0},{3,1},{12,14},{13,15},{10,8},{11,9},{20,22},{21,... | collective-permute-start | bytes 4718600 | tf_op jit(solution)/shard_map/ppermute | solution.py:549
  171.4 56.3 %collective-permute-start.37 = (bf16[8,3,64,512]{3,2,1,0:T(8,128)(2,1)}, bf16[8,3,64,512]{3,2,1,0:T(8,128)(2,1)}, u32[]{:S(2)}, u32[]{:S(2)}) collective-permute-start(bf16[8,3,64,512]{3,2,1,0:T(8,128)(2,1)} %get-tuple-element.260), channel_id=1, source_target_pairs={{2,4},{3,5},{4,2},{5,3},{10,12},{11,13},{12,10},{13,11},{18,20},{1... | collective-permute-start | bytes 4718600 | tf_op jit(solution)/shard_map/ppermute | solution.py:543
  195.0 41.7 %collective-permute-start.31 = (bf16[8,3,64,512]{3,2,1,0:T(8,128)(2,1)}, bf16[8,3,64,512]{3,2,1,0:T(8,128)(2,1)}, u32[]{:S(2)}, u32[]{:S(2)}) collective-permute-start(bf16[8,3,64,512]{3,2,1,0:T(8,128)(2,1)} %get-tuple-element.246), channel_id=1, source_target_pairs={{4,6},{5,7},{2,0},{3,1},{12,14},{13,15},{10,8},{11,9},{20,22},{21,... | collective-permute-start | bytes 4718600 | tf_op jit(solution)/shard_map/ppermute | solution.py:549
  196.7 24.6 %collective-permute-start.39 = (bf16[4,3,64,512]{3,2,1,0:T(8,128)(2,1)S(1)}, bf16[4,3,64,512]{3,2,1,0:T(8,128)(2,1)S(1)}, u32[]{:S(2)}, u32[]{:S(2)}) collective-permute-start(bf16[4,3,64,512]{3,2,1,0:T(8,128)(2,1)S(1)} %get-tuple-element.263.refs_0_), channel_id=1, source_target_pairs={{0,2},{1,3},{6,4},{7,5},{8,10},{9,11},{14,12},{15,13},{16,18},{17,... | collective-permute-start | bytes 2359304 | tf_op jit(solution)/shard_map/ppermute | solution.py:537
  223.6 25.4 %collective-permute-start.41 = (bf16[4,3,64,512]{3,2,1,0:T(8,128)(2,1)S(1)}, bf16[4,3,64,512]{3,2,1,0:T(8,128)(2,1)S(1)}, u32[]{:S(2)}, u32[]{:S(2)}) collective-permute-start(bf16[4,3,64,512]{3,2,1,0:T(8,128)(2,1)S(1)} %get-tuple-element.270.refs_0_), channel_id=1, source_target_pairs={{0,2},{1,3},{6,4},{7,5},{8,10},{9,11},{14,12},{15,13},{16,18},{17,... | collective-permute-start | bytes 2359304 | tf_op jit(solution)/shard_map/ppermute | solution.py:537
  229.5 51.2 %collective-permute-start.48 = (bf16[8,3,64,512]{3,2,1,0:T(8,128)(2,1)}, bf16[8,3,64,512]{3,2,1,0:T(8,128)(2,1)}, u32[]{:S(2)}, u32[]{:S(2)}) collective-permute-start(bf16[8,3,64,512]{3,2,1,0:T(8,128)(2,1)} %get-tuple-element.288), channel_id=1, source_target_pairs={{4,6},{5,7},{2,0},{3,1},{12,14},{13,15},{10,8},{11,9},{20,22},{21,... | collective-permute-start | bytes 4718600 | tf_op jit(solution)/shard_map/ppermute | solution.py:549
  230.8 42.6 %collective-permute-start.44 = (bf16[8,3,64,512]{3,2,1,0:T(8,128)(2,1)}, bf16[8,3,64,512]{3,2,1,0:T(8,128)(2,1)}, u32[]{:S(2)}, u32[]{:S(2)}) collective-permute-start(bf16[8,3,64,512]{3,2,1,0:T(8,128)(2,1)} %get-tuple-element.279), channel_id=1, source_target_pairs={{2,4},{3,5},{4,2},{5,3},{10,12},{11,13},{12,10},{13,11},{18,20},{1... | collective-permute-start | bytes 4718600 | tf_op jit(solution)/shard_map/ppermute | solution.py:543
  251.0 58.2 %collective-permute-start.50 = (bf16[8,3,64,512]{3,2,1,0:T(8,128)(2,1)}, bf16[8,3,64,512]{3,2,1,0:T(8,128)(2,1)}, u32[]{:S(2)}, u32[]{:S(2)}) collective-permute-start(bf16[8,3,64,512]{3,2,1,0:T(8,128)(2,1)} %get-tuple-element.294), channel_id=1, source_target_pairs={{2,4},{3,5},{4,2},{5,3},{10,12},{11,13},{12,10},{13,11},{18,20},{1... | collective-permute-start | bytes 4718600 | tf_op jit(solution)/shard_map/ppermute | solution.py:543
  275.3 46.1 %collective-permute-start.53 = (bf16[8,3,64,512]{3,2,1,0:T(8,128)(2,1)}, bf16[8,3,64,512]{3,2,1,0:T(8,128)(2,1)}, u32[]{:S(2)}, u32[]{:S(2)}) collective-permute-start(bf16[8,3,64,512]{3,2,1,0:T(8,128)(2,1)} %get-tuple-element.301), channel_id=1, source_target_pairs={{4,6},{5,7},{2,0},{3,1},{12,14},{13,15},{10,8},{11,9},{20,22},{21,... | collective-permute-start | bytes 4718600 | tf_op jit(solution)/shard_map/ppermute | solution.py:549
  284.0 42.2 %collective-permute-start.56 = (bf16[8,3,64,256]{3,2,1,0:T(8,128)(2,1)}, bf16[8,3,64,256]{3,2,1,0:T(8,128)(2,1)}, u32[]{:S(2)}, u32[]{:S(2)}) collective-permute-start(bf16[8,3,64,256]{3,2,1,0:T(8,128)(2,1)} %get-tuple-element.306), channel_id=1, source_target_pairs={{2,4},{3,5},{4,2},{5,3},{10,12},{11,13},{12,10},{13,11},{18,20},{1... | collective-permute-start | bytes 2359304 | tf_op jit(solution)/shard_map/ppermute | solution.py:543
  320.2 39.2 %collective-permute-start.58 = (bf16[8,3,64,512]{3,2,1,0:T(8,128)(2,1)S(1)}, bf16[8,3,64,512]{3,2,1,0:T(8,128)(2,1)S(1)}, u32[]{:S(2)}, u32[]{:S(2)}) collective-permute-start(bf16[8,3,64,512]{3,2,1,0:T(8,128)(2,1)S(1)} %get-tuple-element.312), channel_id=1, source_target_pairs={{4,6},{5,7},{2,0},{3,1},{12,14},{13,15},{10,8},{11,9},{20,22},{21,... | collective-permute-start | bytes 4718600 | tf_op jit(solution)/shard_map/ppermute | solution.py:549
  327.0 49.3 %collective-permute-start.60 = (bf16[8,3,64,256]{3,2,1,0:T(8,128)(2,1)S(1)}, bf16[8,3,64,256]{3,2,1,0:T(8,128)(2,1)S(1)}, u32[]{:S(2)}, u32[]{:S(2)}) collective-permute-start(bf16[8,3,64,256]{3,2,1,0:T(8,128)(2,1)S(1)} %get-tuple-element.315), channel_id=1, source_target_pairs={{4,6},{5,7},{2,0},{3,1},{12,14},{13,15},{10,8},{11,9},{20,22},{21,... | collective-permute-start | bytes 2359304 | tf_op jit(solution)/shard_map/ppermute | solution.py:549
  342.7 45.9 %collective-permute-start.57 = (bf16[8,3,64,256]{3,2,1,0:T(8,128)(2,1)S(1)}, bf16[8,3,64,256]{3,2,1,0:T(8,128)(2,1)S(1)}, u32[]{:S(2)}, u32[]{:S(2)}) collective-permute-start(bf16[8,3,64,256]{3,2,1,0:T(8,128)(2,1)S(1)} %get-tuple-element.311), channel_id=1, source_target_pairs={{4,6},{5,7},{2,0},{3,1},{12,14},{13,15},{10,8},{11,9},{20,22},{21,... | collective-permute-start | bytes 2359304 | tf_op jit(solution)/shard_map/ppermute | solution.py:549
  (59 other events, 651.8 us)

commit v4 on v3

--- a/solution.py
+++ b/solution.py
@@ -228,60 +228,58 @@
     return rows.reshape(2, 2 * experts * KINDS * block_rows, depth)
 
 
-def product(here_ref, lhs_ref, rot_ref, tile_ref, sems, column):
-    step, total = pl.program_id(0), pl.num_programs(0)
+def each_tile(lhs, rot_ref, tile_ref, sems, column, width, use):
+    total = width // TILE
 
     def tile_copy(index):
         slot = lax.rem(index, 2)
         columns = pl.ds(pl.multiple_of(column + index * TILE, TILE), TILE)
         return pltpu.make_async_copy(rot_ref.at[:, columns], tile_ref.at[slot], sems.at[slot])
 
-    @pl.when(step == 0)
-    def _():
-        tile_copy(step).start()
-
-    @pl.when(step + 1 < total)
-    def _():
-        tile_copy(step + 1).start()
-
-    tile_copy(step).wait()
-    return jnp.dot(
-        lhs_ref[0], tile_ref[lax.rem(step, 2)], preferred_element_type=jnp.float32
-    )
+    tile_copy(0).start()
+
+    @pl.loop(0, total)
+    def _(index):
+        @pl.when(index + 1 < total)
+        def _():
+            tile_copy(index + 1).start()
+
+        tile_copy(index).wait()
+        result = jnp.dot(
+            lhs[...], tile_ref[lax.rem(index, 2)], preferred_element_type=jnp.float32
+        )
+        use(pl.ds(pl.multiple_of(index * TILE, TILE), TILE), result)
 
 
 def send_kernel(here_ref, lhs_ref, rot_ref, after_ref, out_ref, mark_ref, *scratch, column):
-    total = product(here_ref, lhs_ref, rot_ref, *scratch, column)
-    out_ref[...] = total.astype(jnp.bfloat16)
+    def use(columns, result):
+        out_ref[:, columns] = result.astype(jnp.bfloat16)
+
+    lhs = lhs_ref.at[1 - here_ref[0] % 2]
+    each_tile(lhs, rot_ref, *scratch, column, out_ref.shape[1], use)
 
 
 def keep_kernel(
     here_ref, lhs_ref, rot_ref, recv_ref, after_ref, away_ref, home_ref, mark_ref, *scratch, column
 ):
-    rows = away_ref.shape[0]
-    total = product(here_ref, lhs_ref, rot_ref, *scratch, column)
-    total = (total + recv_ref[...].astype(jnp.float32)).astype(jnp.bfloat16)
+    rows, width = away_ref.shape
     x = here_ref[0] // 2
 
-    @pl.when(x == 0)
-    def _():
-        home_ref[...] = total[:rows]
-        away_ref[...] = total[rows:]
-
-    @pl.when(x == 1)
-    def _():
-        home_ref[...] = total[rows:]
-        away_ref[...] = total[:rows]
-
-
-def lhs_spec(lhs, send):
-    _, rows, depth = lhs.shape
-
-    def lhs_map(tile, here):
-        core = here[0] % 2
-        return (1 - core if send else core, 0, 0)
-
-    return pl.BlockSpec((1, rows, depth), lhs_map, pipeline_mode=pl.Buffered(1))
+    def use(columns, result):
+        total = (result + recv_ref[:, columns].astype(jnp.float32)).astype(jnp.bfloat16)
+
+        @pl.when(x == 0)
+        def _():
+            home_ref[:, columns] = total[:rows]
+            away_ref[:, columns] = total[rows:]
+
+        @pl.when(x == 1)
+        def _():
+            home_ref[:, columns] = total[rows:]
+            away_ref[:, columns] = total[:rows]
+
+    lhs = lhs_ref.at[here_ref[0] % 2]
+    each_tile(lhs, rot_ref, *scratch, column, width, use)
 
 
 def tile_scratch(depth):
@@ -293,13 +291,9 @@
     return pl.pallas_call(
         functools.partial(send_kernel, column=column),
         out_shape=(jax.ShapeDtypeStruct((rows, width), jnp.bfloat16), MARK),
-        grid_spec=pltpu.PrefetchScalarGridSpec(
-            num_scalar_prefetch=1,
-            grid=(width // TILE,),
-            in_specs=[lhs_spec(lhs, True), ON_HBM, ANYWHERE],
-            out_specs=(pl.BlockSpec((rows, TILE), lambda t, here: (0, t)), ANYWHERE),
-            scratch_shapes=tile_scratch(depth),
-        ),
+        in_specs=[ON_SMEM, ON_VMEM, ON_HBM, ANYWHERE],
+        out_specs=(ON_VMEM, ANYWHERE),
+        scratch_shapes=tile_scratch(depth),
         compiler_params=pltpu.CompilerParams(vmem_limit_bytes=MATMUL_VMEM),
         cost_estimate=cost,
         name="matmul_send",
@@ -309,18 +303,12 @@
 def matmul_keep(here, lhs, rotation, recv, column, width, after, cost):
     _, rows, depth = lhs.shape
     out = jax.ShapeDtypeStruct((rows // 2, width), jnp.bfloat16)
-    out_spec = pl.BlockSpec((rows // 2, TILE), lambda t, here: (0, t))
-    recv_spec = pl.BlockSpec((rows, TILE), lambda t, here: (0, t))
     return pl.pallas_call(
         functools.partial(keep_kernel, column=column),
         out_shape=(out, out, MARK),
-        grid_spec=pltpu.PrefetchScalarGridSpec(
-            num_scalar_prefetch=1,
-            grid=(width // TILE,),
-            in_specs=[lhs_spec(lhs, False), ON_HBM, recv_spec, ANYWHERE],
-            out_specs=(out_spec, out_spec, ANYWHERE),
-            scratch_shapes=tile_scratch(depth),
-        ),
+        in_specs=[ON_SMEM, ON_VMEM, ON_HBM, ON_VMEM, ANYWHERE],
+        out_specs=(ON_VMEM, ON_VMEM, ANYWHERE),
+        scratch_shapes=tile_scratch(depth),
         compiler_params=pltpu.CompilerParams(vmem_limit_bytes=MATMUL_VMEM),
         cost_estimate=cost,
         name="matmul_keep",

time: 403 us -> 398 us (0.988)
  Pallas kernels: 172 us -> 163 us
  starting transfers between devices: 107 us -> 113 us
    pallas_call x9, Pallas kernels: 28.4 us -> 23.7 us  [place(): pl.pallas_call(functools.partial(place_kernel, bases=bases, column=column...]
  transfers between devices with their start and end apart: 63 -> 63, of which waited for: 17 -> 17; matrix products, arithmetic and copies ran while one was open for 0% -> 0% of each run, Pallas kernels for 40% -> 38%
where the time goes in v4:
time: 398 us; the launch traced here: 396 us
  Pallas kernels  163 us (41%)
  waiting for transfers between devices  114 us (29%)
  starting transfers between devices  113 us (28%)
  local copies, waits for them, and re-layouts  5.16 us (1%)
    ppermute x9, starting transfers between devices, send_inward(): far[i] = lax.ppermute(near[i], 'ep', inward)  47 us
    pallas_call x9, Pallas kernels, matmul_keep(): pl.pallas_call(functools.partial(keep_kernel, column=column), out_shape=(...  44.3 us
    pallas_call x9, Pallas kernels, matmul_send(): pl.pallas_call(functools.partial(send_kernel, column=column), out_shape=(...  42.3 us
    ppermute x9, waiting for transfers between devices, send_outward(): outer[i] = lax.ppermute(out, 'ep', outward)  40.9 us
    ppermute x9, waiting for transfers between devices, send_partner(): partner[i] = lax.ppermute(out, 'ep', along_y)  40.6 us
    pallas_call x27, Pallas kernels, pick(): pl.pallas_call(functools.partial(pick_kernel, first=first, bases=bases),...  35.5 us
    pallas_call x9, Pallas kernels, place(): pl.pallas_call(functools.partial(place_kernel, bases=bases, column=column...  23.7 us
    ppermute x9, starting transfers between devices, send_partner(): partner[i] = lax.ppermute(out, 'ep', along_y)  14.8 us
  transfers between devices with their start and end apart: 63, of which 17 were waited for; matrix products, arithmetic and copies ran while one was open for 0% of the time, Pallas kernels for 38%

profile of v4, /device:TPU:0, one launch (start us, length us, event | category | flops | bytes accessed | tf_op | source)
XLA Modules:
  0.0 396.2 jit_solution(1496823804373325408)
XLA Ops:
  22.2 5.7 %matmul_send.11 = (bf16[768,1024]{1,0:T(8,128)(2,1)S(1)}, f32[8,128]{1,0:T(8,128)S(1)}) custom-call(s32[2]{0:T(128)S(1)} %pad_add_fusion.here_ref.after_ref, bf16[2,768,1792]{2,1,0:T(8,128)(2,1)S(1)} %bitcast.27, bf16[1792,7168]{1,0:T(8,128)(2,1)} %rot_ref.35, f32[8,128]{1,0:T(8,128)S(1)} %get-tuple-element.171.after_ref), custom_call_target="tpu_custom_call" | custom-call | flops 24999999488 | bytes 1024 | tf_op jit(solution)/shard_map/matmul_send/pallas_call | solution.py:291
  32.1 6.7 %matmul_keep.11 = (bf16[384,1024]{1,0:T(8,128)(2,1)}, bf16[384,1024]{1,0:T(8,128)(2,1)S(1)}, f32[8,128]{1,0:T(8,128)S(1)}) custom-call(s32[2]{0:T(128)S(1)} %pad_add_fusion.here_ref.after_ref, bf16[2,768,1792]{2,1,0:T(8,128)(2,1)S(1)} %bitcast.29, bf16[1792,7168]{1,0:T(8,128)(2,1)} %rot_ref.35, bf16[768,1024]{1,0:T(8,128)(2,1)S(1)} %collective-permute-done.2.recv_ref, ...), custom_call_target="tpu_custom_call" | custom-call | flops 24999999488 | bytes 1024 | tf_op jit(solution)/shard_map/matmul_keep/pallas_call | solution.py:306
  43.1 5.6 %matmul_send.12 = (bf16[768,1024]{1,0:T(8,128)(2,1)S(1)}, f32[8,128]{1,0:T(8,128)S(1)}) custom-call(s32[2]{0:T(128)S(1)} %pad_add_fusion.here_ref.after_ref, bf16[2,768,1792]{2,1,0:T(8,128)(2,1)S(1)} %bitcast.30, bf16[1792,7168]{1,0:T(8,128)(2,1)} %rot_ref.35, f32[8,128]{1,0:T(8,128)S(1)} %get-tuple-element.177.after_ref), custom_call_target="tpu_custom_call" | custom-call | flops 24999999488 | bytes 1024 | tf_op jit(solution)/shard_map/matmul_send/pallas_call | solution.py:291
  54.2 5.8 %matmul_keep.12 = (bf16[384,1024]{1,0:T(8,128)(2,1)S(1)}, bf16[384,1024]{1,0:T(8,128)(2,1)S(1)}, f32[8,128]{1,0:T(8,128)S(1)}) custom-call(s32[2]{0:T(128)S(1)} %pad_add_fusion.here_ref.after_ref, bf16[2,768,1792]{2,1,0:T(8,128)(2,1)S(1)} %bitcast.31, bf16[1792,7168]{1,0:T(8,128)(2,1)} %rot_ref.35, bf16[768,1024]{1,0:T(8,128)(2,1)S(1)} %collective-permute-done.4.recv_ref, ...), custom_call_target="tpu_custom_call" | custom-call | flops 24999999488 | bytes 1024 | tf_op jit(solution)/shard_map/matmul_keep/pallas_call | solution.py:306
  69.7 5.6 %matmul_send.13 = (bf16[768,1024]{1,0:T(8,128)(2,1)S(1)}, f32[8,128]{1,0:T(8,128)S(1)}) custom-call(s32[2]{0:T(128)S(1)} %pad_add_fusion.here_ref.after_ref, bf16[2,768,1792]{2,1,0:T(8,128)(2,1)S(1)} %bitcast.32, bf16[1792,7168]{1,0:T(8,128)(2,1)} %rot_ref.35, f32[8,128]{1,0:T(8,128)S(1)} %get-tuple-element.197.after_ref), custom_call_target="tpu_custom_call" | custom-call | flops 24999999488 | bytes 1024 | tf_op jit(solution)/shard_map/matmul_send/pallas_call | solution.py:291
  78.2 5.8 %collective-permute-start.16 = (bf16[4,3,64,512]{3,2,1,0:T(8,128)(2,1)S(1)}, bf16[4,3,64,512]{3,2,1,0:T(8,128)(2,1)S(1)}, u32[]{:S(2)}, u32[]{:S(2)}) collective-permute-start(bf16[4,3,64,512]{3,2,1,0:T(8,128)(2,1)S(1)} %get-tuple-element.209.refs_0_), channel_id=1, source_target_pairs={{0,2},{1,3},{6,4},{7,5},{8,10},{9,11},{14,12},{15,13},{16,18},{17,... | collective-permute-start | bytes 2359304 | tf_op jit(solution)/shard_map/ppermute | solution.py:525
  84.7 5.8 %matmul_keep.13 = (bf16[384,1024]{1,0:T(8,128)(2,1)S(1)}, bf16[384,1024]{1,0:T(8,128)(2,1)S(1)}, f32[8,128]{1,0:T(8,128)S(1)}) custom-call(s32[2]{0:T(128)S(1)} %pad_add_fusion.here_ref.after_ref, bf16[2,768,1792]{2,1,0:T(8,128)(2,1)S(1)} %bitcast.33, bf16[1792,7168]{1,0:T(8,128)(2,1)} %rot_ref.35, bf16[768,1024]{1,0:T(8,128)(2,1)S(1)} %collective-permute-done.12.recv_ref, ...), custom_call_target="tpu_custom_call" | custom-call | flops 24999999488 | bytes 1024 | tf_op jit(solution)/shard_map/matmul_keep/pallas_call | solution.py:306
  95.6 5.8 %collective-permute-done.16.refs_1_ = bf16[4,3,64,512]{3,2,1,0:T(8,128)(2,1)S(1)} collective-permute-done((bf16[4,3,64,512]{3,2,1,0:T(8,128)(2,1)S(1)}, bf16[4,3,64,512]{3,2,1,0:T(8,128)(2,1)S(1)}, u32[]{:S(2)}, u32[]{:S(2)}) %collective-permute-start.16) | collective-permute-done | bytes 786464 | tf_op jit(solution)/shard_map/ppermute | solution.py:525
  117.8 9.0 %collective-permute-done.20.side_ref = bf16[2,3,64,512]{3,2,1,0:T(8,128)(2,1)S(1)} collective-permute-done((bf16[2,3,64,512]{3,2,1,0:T(8,128)(2,1)S(1)}, bf16[2,3,64,512]{3,2,1,0:T(8,128)(2,1)S(1)}, u32[]{:S(2)}, u32[]{:S(2)}) %collective-permute-start.20) | collective-permute-done | bytes 393248 | tf_op jit(solution)/shard_map/ppermute | solution.py:520
  141.5 5.7 %matmul_send.14 = (bf16[768,1024]{1,0:T(8,128)(2,1)S(1)}, f32[8,128]{1,0:T(8,128)S(1)}) custom-call(s32[2]{0:T(128)S(1)} %pad_add_fusion.here_ref.after_ref, bf16[2,768,1792]{2,1,0:T(8,128)(2,1)S(1)} %bitcast.34, bf16[1792,7168]{1,0:T(8,128)(2,1)} %rot_ref.35, f32[8,128]{1,0:T(8,128)S(1)} %get-tuple-element.229.after_ref), custom_call_target="tpu_custom_call" | custom-call | flops 24999999488 | bytes 1024 | tf_op jit(solution)/shard_map/matmul_send/pallas_call | solution.py:291
  152.7 5.8 %matmul_keep.14 = (bf16[384,1024]{1,0:T(8,128)(2,1)S(1)}, bf16[384,1024]{1,0:T(8,128)(2,1)S(1)}, f32[8,128]{1,0:T(8,128)S(1)}) custom-call(s32[2]{0:T(128)S(1)} %pad_add_fusion.here_ref.after_ref, bf16[2,768,1792]{2,1,0:T(8,128)(2,1)S(1)} %bitcast.35, bf16[1792,7168]{1,0:T(8,128)(2,1)} %rot_ref.35, bf16[768,1024]{1,0:T(8,128)(2,1)S(1)} %collective-permute-done.25.recv_ref, ...), custom_call_target="tpu_custom_call" | custom-call | flops 24999999488 | bytes 1024 | tf_op jit(solution)/shard_map/matmul_keep/pallas_call | solution.py:306
  160.2 5.6 %matmul_send.15 = (bf16[768,1024]{1,0:T(8,128)(2,1)S(1)}, f32[8,128]{1,0:T(8,128)S(1)}) custom-call(s32[2]{0:T(128)S(1)} %pad_add_fusion.here_ref.after_ref, bf16[2,768,1792]{2,1,0:T(8,128)(2,1)S(1)} %bitcast.36, bf16[1792,7168]{1,0:T(8,128)(2,1)} %rot_ref.35, f32[8,128]{1,0:T(8,128)S(1)} %get-tuple-element.239.after_ref), custom_call_target="tpu_custom_call" | custom-call | flops 24999999488 | bytes 1024 | tf_op jit(solution)/shard_map/matmul_send/pallas_call | solution.py:291
  169.8 5.8 %matmul_keep.15 = (bf16[384,1024]{1,0:T(8,128)(2,1)S(1)}, bf16[384,1024]{1,0:T(8,128)(2,1)S(1)}, f32[8,128]{1,0:T(8,128)S(1)}) custom-call(s32[2]{0:T(128)S(1)} %pad_add_fusion.here_ref.after_ref, bf16[2,768,1792]{2,1,0:T(8,128)(2,1)S(1)} %bitcast.37, bf16[1792,7168]{1,0:T(8,128)(2,1)} %rot_ref.35, bf16[768,1024]{1,0:T(8,128)(2,1)S(1)} %collective-permute-done.29.recv_ref, ...), custom_call_target="tpu_custom_call" | custom-call | flops 24999999488 | bytes 1024 | tf_op jit(solution)/shard_map/matmul_keep/pallas_call | solution.py:306
  193.4 5.7 %collective-permute-start.39 = (bf16[4,3,64,512]{3,2,1,0:T(8,128)(2,1)S(1)}, bf16[4,3,64,512]{3,2,1,0:T(8,128)(2,1)S(1)}, u32[]{:S(2)}, u32[]{:S(2)}) collective-permute-start(bf16[4,3,64,512]{3,2,1,0:T(8,128)(2,1)S(1)} %get-tuple-element.263.refs_0_), channel_id=1, source_target_pairs={{0,2},{1,3},{6,4},{7,5},{8,10},{9,11},{14,12},{15,13},{16,18},{17,... | collective-permute-start | bytes 2359304 | tf_op jit(solution)/shard_map/ppermute | solution.py:525
  201.1 9.5 %collective-permute-done.33.refs_4_ = bf16[4,3,64,512]{3,2,1,0:T(8,128)(2,1)S(1)} collective-permute-done((bf16[4,3,64,512]{3,2,1,0:T(8,128)(2,1)S(1)}, bf16[4,3,64,512]{3,2,1,0:T(8,128)(2,1)S(1)}, u32[]{:S(2)}, u32[]{:S(2)}) %collective-permute-start.33) | collective-permute-done | bytes 786464 | tf_op jit(solution)/shard_map/ppermute | solution.py:543
  237.1 6.9 %collective-permute-done.42.recv_ref = bf16[384,512]{1,0:T(8,128)(2,1)S(1)} collective-permute-done((bf16[384,512]{1,0:T(8,128)(2,1)S(1)}, bf16[384,512]{1,0:T(8,128)(2,1)S(1)}, u32[]{:S(2)}, u32[]{:S(2)}) %collective-permute-start.42) | collective-permute-done | bytes 393248 | tf_op jit(solution)/shard_map/ppermute | solution.py:513
  250.6 5.6 %collective-permute-done.40.refs_4_ = bf16[4,3,64,512]{3,2,1,0:T(8,128)(2,1)S(1)} collective-permute-done((bf16[4,3,64,512]{3,2,1,0:T(8,128)(2,1)S(1)}, bf16[4,3,64,512]{3,2,1,0:T(8,128)(2,1)S(1)}, u32[]{:S(2)}, u32[]{:S(2)}) %collective-permute-start.40) | collective-permute-done | bytes 786464 | tf_op jit(solution)/shard_map/ppermute | solution.py:543
  263.3 6.9 %collective-permute-start.47 = (bf16[4,3,64,256]{3,2,1,0:T(8,128)(2,1)S(1)}, bf16[4,3,64,256]{3,2,1,0:T(8,128)(2,1)S(1)}, u32[]{:S(2)}, u32[]{:S(2)}) collective-permute-start(bf16[4,3,64,256]{3,2,1,0:T(8,128)(2,1)S(1)} %get-tuple-element.287.refs_0_), channel_id=1, source_target_pairs={{0,2},{1,3},{6,4},{7,5},{8,10},{9,11},{14,12},{15,13},{16,18},{17,... | collective-permute-start | bytes 1179656 | tf_op jit(solution)/shard_map/ppermute | solution.py:525
  291.8 11.7 %collective-permute-done.51.refs_4_ = bf16[4,3,64,512]{3,2,1,0:T(8,128)(2,1)S(1)} collective-permute-done((bf16[4,3,64,512]{3,2,1,0:T(8,128)(2,1)S(1)}, bf16[4,3,64,512]{3,2,1,0:T(8,128)(2,1)S(1)}, u32[]{:S(2)}, u32[]{:S(2)}) %collective-permute-start.51) | collective-permute-done | bytes 786464 | tf_op jit(solution)/shard_map/ppermute | solution.py:543
  307.6 7.7 %collective-permute-start.52 = (bf16[4,3,64,256]{3,2,1,0:T(8,128)(2,1)S(1)}, bf16[4,3,64,256]{3,2,1,0:T(8,128)(2,1)S(1)}, u32[]{:S(2)}, u32[]{:S(2)}) collective-permute-start(bf16[4,3,64,256]{3,2,1,0:T(8,128)(2,1)S(1)} %get-tuple-element.300.refs_0_), channel_id=1, source_target_pairs={{0,2},{1,3},{6,4},{7,5},{8,10},{9,11},{14,12},{15,13},{16,18},{17,... | collective-permute-start | bytes 1179656 | tf_op jit(solution)/shard_map/ppermute | solution.py:525
  325.5 10.0 %collective-permute-done.55.refs_4_ = bf16[4,3,64,512]{3,2,1,0:T(8,128)(2,1)S(1)} collective-permute-done((bf16[4,3,64,512]{3,2,1,0:T(8,128)(2,1)S(1)}, bf16[4,3,64,512]{3,2,1,0:T(8,128)(2,1)S(1)}, u32[]{:S(2)}, u32[]{:S(2)}) %collective-permute-start.55) | collective-permute-done | bytes 786464 | tf_op jit(solution)/shard_map/ppermute | solution.py:543
  340.6 14.0 %collective-permute-done.58.refs_3_ = bf16[8,3,64,512]{3,2,1,0:T(8,128)(2,1)S(1)} collective-permute-done((bf16[8,3,64,512]{3,2,1,0:T(8,128)(2,1)S(1)}, bf16[8,3,64,512]{3,2,1,0:T(8,128)(2,1)S(1)}, u32[]{:S(2)}, u32[]{:S(2)}) %collective-permute-start.58) | collective-permute-done | bytes 1572896 | tf_op jit(solution)/shard_map/ppermute | solution.py:537
  357.7 13.8 %collective-permute-done.60.refs_3_ = bf16[8,3,64,256]{3,2,1,0:T(8,128)(2,1)S(1)} collective-permute-done((bf16[8,3,64,256]{3,2,1,0:T(8,128)(2,1)S(1)}, bf16[8,3,64,256]{3,2,1,0:T(8,128)(2,1)S(1)}, u32[]{:S(2)}, u32[]{:S(2)}) %collective-permute-start.60) | collective-permute-done | bytes 786464 | tf_op jit(solution)/shard_map/ppermute | solution.py:537
  377.3 7.8 %collective-permute-done.57.refs_3_ = bf16[8,3,64,256]{3,2,1,0:T(8,128)(2,1)S(1)} collective-permute-done((bf16[8,3,64,256]{3,2,1,0:T(8,128)(2,1)S(1)}, bf16[8,3,64,256]{3,2,1,0:T(8,128)(2,1)S(1)}, u32[]{:S(2)}, u32[]{:S(2)}) %collective-permute-start.57) | collective-permute-done | bytes 786464 | tf_op jit(solution)/shard_map/ppermute | solution.py:537
  (217 shorter events, 216.3 us)
Async XLA Ops:
  15.7 23.1 %collective-permute-start.1 = (bf16[384,512]{1,0:T(8,128)(2,1)S(1)}, bf16[384,512]{1,0:T(8,128)(2,1)S(1)}, u32[]{:S(2)}, u32[]{:S(2)}) collective-permute-start(bf16[384,512]{1,0:T(8,128)(2,1)S(1)} %get-tuple-element.169), channel_id=1, source_target_pairs={{0,16},{8,24},{16,0},{24,8},{1,17},{9,25},{17,1},{25,9},{2,18},{10... | collective-permute-start | bytes 1179656 | tf_op jit(solution)/shard_map/ppermute | solution.py:513
  41.6 22.6 %collective-permute-start.11 = (bf16[384,1024]{1,0:T(8,128)(2,1)}, bf16[384,1024]{1,0:T(8,128)(2,1)}, u32[]{:S(2)}, u32[]{:S(2)}) collective-permute-start(bf16[384,1024]{1,0:T(8,128)(2,1)} %get-tuple-element.195), channel_id=1, source_target_pairs={{0,16},{8,24},{16,0},{24,8},{1,17},{9,25},{17,1},{25,9},{2,18},{10... | collective-permute-start | bytes 2359304 | tf_op jit(solution)/shard_map/ppermute | solution.py:513
  69.1 22.2 %collective-permute-start.7 = (bf16[384,1024]{1,0:T(8,128)(2,1)S(1)}, bf16[384,1024]{1,0:T(8,128)(2,1)S(1)}, u32[]{:S(2)}, u32[]{:S(2)}) collective-permute-start(bf16[384,1024]{1,0:T(8,128)(2,1)S(1)} %get-tuple-element.187), channel_id=1, source_target_pairs={{0,16},{8,24},{16,0},{24,8},{1,17},{9,25},{17,1},{25,9},{2,18},{10... | collective-permute-start | bytes 2359304 | tf_op jit(solution)/shard_map/ppermute | solution.py:513
  78.2 23.2 %collective-permute-start.16 = (bf16[4,3,64,512]{3,2,1,0:T(8,128)(2,1)S(1)}, bf16[4,3,64,512]{3,2,1,0:T(8,128)(2,1)S(1)}, u32[]{:S(2)}, u32[]{:S(2)}) collective-permute-start(bf16[4,3,64,512]{3,2,1,0:T(8,128)(2,1)S(1)} %get-tuple-element.209.refs_0_), channel_id=1, source_target_pairs={{0,2},{1,3},{6,4},{7,5},{8,10},{9,11},{14,12},{15,13},{16,18},{17,... | collective-permute-start | bytes 2359304 | tf_op jit(solution)/shard_map/ppermute | solution.py:525
  92.7 23.1 %collective-permute-start.21 = (bf16[8,3,64,256]{3,2,1,0:T(8,128)(2,1)S(1)}, bf16[8,3,64,256]{3,2,1,0:T(8,128)(2,1)S(1)}, u32[]{:S(2)}, u32[]{:S(2)}) collective-permute-start(bf16[8,3,64,256]{3,2,1,0:T(8,128)(2,1)S(1)} %get-tuple-element.220), channel_id=1, source_target_pairs={{4,6},{5,7},{2,0},{3,1},{12,14},{13,15},{10,8},{11,9},{20,22},{21,... | collective-permute-start | bytes 2359304 | tf_op jit(solution)/shard_map/ppermute | solution.py:537
  103.3 43.9 %collective-permute-start.27 = (bf16[8,3,64,512]{3,2,1,0:T(8,128)(2,1)}, bf16[8,3,64,512]{3,2,1,0:T(8,128)(2,1)}, u32[]{:S(2)}, u32[]{:S(2)}) collective-permute-start(bf16[8,3,64,512]{3,2,1,0:T(8,128)(2,1)} %get-tuple-element.232), channel_id=1, source_target_pairs={{2,4},{3,5},{4,2},{5,3},{10,12},{11,13},{12,10},{13,11},{18,20},{1... | collective-permute-start | bytes 4718600 | tf_op jit(solution)/shard_map/ppermute | solution.py:531
  107.0 27.9 %collective-permute-start.24 = (bf16[8,3,64,256]{3,2,1,0:T(8,128)(2,1)S(1)}, bf16[8,3,64,256]{3,2,1,0:T(8,128)(2,1)S(1)}, u32[]{:S(2)}, u32[]{:S(2)}) collective-permute-start(bf16[8,3,64,256]{3,2,1,0:T(8,128)(2,1)S(1)} %get-tuple-element.226), channel_id=1, source_target_pairs={{4,6},{5,7},{2,0},{3,1},{12,14},{13,15},{10,8},{11,9},{20,22},{21,... | collective-permute-start | bytes 2359304 | tf_op jit(solution)/shard_map/ppermute | solution.py:537
  108.5 24.4 %collective-permute-start.17 = (bf16[4,3,64,512]{3,2,1,0:T(8,128)(2,1)S(1)}, bf16[4,3,64,512]{3,2,1,0:T(8,128)(2,1)S(1)}, u32[]{:S(2)}, u32[]{:S(2)}) collective-permute-start(bf16[4,3,64,512]{3,2,1,0:T(8,128)(2,1)S(1)} %get-tuple-element.212.refs_0_), channel_id=1, source_target_pairs={{0,2},{1,3},{6,4},{7,5},{8,10},{9,11},{14,12},{15,13},{16,18},{17,... | collective-permute-start | bytes 2359304 | tf_op jit(solution)/shard_map/ppermute | solution.py:525
  116.7 22.6 %collective-permute-start.23 = (bf16[4,3,64,256]{3,2,1,0:T(8,128)(2,1)S(1)}, bf16[4,3,64,256]{3,2,1,0:T(8,128)(2,1)S(1)}, u32[]{:S(2)}, u32[]{:S(2)}) collective-permute-start(bf16[4,3,64,256]{3,2,1,0:T(8,128)(2,1)S(1)} %get-tuple-element.225), channel_id=1, source_target_pairs={{0,1},{1,0},{2,3},{3,2},{4,5},{5,4},{6,7},{7,6},{8,9},{9,8},{10,11... | collective-permute-start | bytes 1179656 | tf_op jit(solution)/shard_map/ppermute | solution.py:543
  128.0 38.1 %collective-permute-start.30 = (bf16[4,3,64,512]{3,2,1,0:T(8,128)(2,1)}, bf16[4,3,64,512]{3,2,1,0:T(8,128)(2,1)}, u32[]{:S(2)}, u32[]{:S(2)}) collective-permute-start(bf16[4,3,64,512]{3,2,1,0:T(8,128)(2,1)} %get-tuple-element.241.refs_0_), channel_id=1, source_target_pairs={{0,2},{1,3},{6,4},{7,5},{8,10},{9,11},{14,12},{15,13},{16,18},{17,... | collective-permute-start | bytes 2359304 | tf_op jit(solution)/shard_map/ppermute | solution.py:525
  137.4 43.8 %collective-permute-start.22 = (bf16[8,3,64,512]{3,2,1,0:T(8,128)(2,1)}, bf16[8,3,64,512]{3,2,1,0:T(8,128)(2,1)}, u32[]{:S(2)}, u32[]{:S(2)}) collective-permute-start(bf16[8,3,64,512]{3,2,1,0:T(8,128)(2,1)} %get-tuple-element.224), channel_id=1, source_target_pairs={{2,4},{3,5},{4,2},{5,3},{10,12},{11,13},{12,10},{13,11},{18,20},{1... | collective-permute-start | bytes 4718600 | tf_op jit(solution)/shard_map/ppermute | solution.py:531
  149.1 39.4 %collective-permute-start.32 = (bf16[8,3,64,512]{3,2,1,0:T(8,128)(2,1)}, bf16[8,3,64,512]{3,2,1,0:T(8,128)(2,1)}, u32[]{:S(2)}, u32[]{:S(2)}) collective-permute-start(bf16[8,3,64,512]{3,2,1,0:T(8,128)(2,1)} %get-tuple-element.247), channel_id=1, source_target_pairs={{4,6},{5,7},{2,0},{3,1},{12,14},{13,15},{10,8},{11,9},{20,22},{21,... | collective-permute-start | bytes 4718600 | tf_op jit(solution)/shard_map/ppermute | solution.py:537
  167.9 55.8 %collective-permute-start.37 = (bf16[8,3,64,512]{3,2,1,0:T(8,128)(2,1)}, bf16[8,3,64,512]{3,2,1,0:T(8,128)(2,1)}, u32[]{:S(2)}, u32[]{:S(2)}) collective-permute-start(bf16[8,3,64,512]{3,2,1,0:T(8,128)(2,1)} %get-tuple-element.260), channel_id=1, source_target_pairs={{2,4},{3,5},{4,2},{5,3},{10,12},{11,13},{12,10},{13,11},{18,20},{1... | collective-permute-start | bytes 4718600 | tf_op jit(solution)/shard_map/ppermute | solution.py:531
  191.7 42.6 %collective-permute-start.31 = (bf16[8,3,64,512]{3,2,1,0:T(8,128)(2,1)}, bf16[8,3,64,512]{3,2,1,0:T(8,128)(2,1)}, u32[]{:S(2)}, u32[]{:S(2)}) collective-permute-start(bf16[8,3,64,512]{3,2,1,0:T(8,128)(2,1)} %get-tuple-element.246), channel_id=1, source_target_pairs={{4,6},{5,7},{2,0},{3,1},{12,14},{13,15},{10,8},{11,9},{20,22},{21,... | collective-permute-start | bytes 4718600 | tf_op jit(solution)/shard_map/ppermute | solution.py:537
  193.4 23.8 %collective-permute-start.39 = (bf16[4,3,64,512]{3,2,1,0:T(8,128)(2,1)S(1)}, bf16[4,3,64,512]{3,2,1,0:T(8,128)(2,1)S(1)}, u32[]{:S(2)}, u32[]{:S(2)}) collective-permute-start(bf16[4,3,64,512]{3,2,1,0:T(8,128)(2,1)S(1)} %get-tuple-element.263.refs_0_), channel_id=1, source_target_pairs={{0,2},{1,3},{6,4},{7,5},{8,10},{9,11},{14,12},{15,13},{16,18},{17,... | collective-permute-start | bytes 2359304 | tf_op jit(solution)/shard_map/ppermute | solution.py:525
  219.5 27.2 %collective-permute-start.41 = (bf16[4,3,64,512]{3,2,1,0:T(8,128)(2,1)S(1)}, bf16[4,3,64,512]{3,2,1,0:T(8,128)(2,1)S(1)}, u32[]{:S(2)}, u32[]{:S(2)}) collective-permute-start(bf16[4,3,64,512]{3,2,1,0:T(8,128)(2,1)S(1)} %get-tuple-element.270.refs_0_), channel_id=1, source_target_pairs={{0,2},{1,3},{6,4},{7,5},{8,10},{9,11},{14,12},{15,13},{16,18},{17,... | collective-permute-start | bytes 2359304 | tf_op jit(solution)/shard_map/ppermute | solution.py:525
  225.6 52.4 %collective-permute-start.48 = (bf16[8,3,64,512]{3,2,1,0:T(8,128)(2,1)}, bf16[8,3,64,512]{3,2,1,0:T(8,128)(2,1)}, u32[]{:S(2)}, u32[]{:S(2)}) collective-permute-start(bf16[8,3,64,512]{3,2,1,0:T(8,128)(2,1)} %get-tuple-element.288), channel_id=1, source_target_pairs={{4,6},{5,7},{2,0},{3,1},{12,14},{13,15},{10,8},{11,9},{20,22},{21,... | collective-permute-start | bytes 4718600 | tf_op jit(solution)/shard_map/ppermute | solution.py:537
  226.9 43.4 %collective-permute-start.44 = (bf16[8,3,64,512]{3,2,1,0:T(8,128)(2,1)}, bf16[8,3,64,512]{3,2,1,0:T(8,128)(2,1)}, u32[]{:S(2)}, u32[]{:S(2)}) collective-permute-start(bf16[8,3,64,512]{3,2,1,0:T(8,128)(2,1)} %get-tuple-element.279), channel_id=1, source_target_pairs={{2,4},{3,5},{4,2},{5,3},{10,12},{11,13},{12,10},{13,11},{18,20},{1... | collective-permute-start | bytes 4718600 | tf_op jit(solution)/shard_map/ppermute | solution.py:531
  248.7 57.6 %collective-permute-start.50 = (bf16[8,3,64,512]{3,2,1,0:T(8,128)(2,1)}, bf16[8,3,64,512]{3,2,1,0:T(8,128)(2,1)}, u32[]{:S(2)}, u32[]{:S(2)}) collective-permute-start(bf16[8,3,64,512]{3,2,1,0:T(8,128)(2,1)} %get-tuple-element.294), channel_id=1, source_target_pairs={{2,4},{3,5},{4,2},{5,3},{10,12},{11,13},{12,10},{13,11},{18,20},{1... | collective-permute-start | bytes 4718600 | tf_op jit(solution)/shard_map/ppermute | solution.py:531
  272.3 44.4 %collective-permute-start.53 = (bf16[8,3,64,512]{3,2,1,0:T(8,128)(2,1)}, bf16[8,3,64,512]{3,2,1,0:T(8,128)(2,1)}, u32[]{:S(2)}, u32[]{:S(2)}) collective-permute-start(bf16[8,3,64,512]{3,2,1,0:T(8,128)(2,1)} %get-tuple-element.301), channel_id=1, source_target_pairs={{4,6},{5,7},{2,0},{3,1},{12,14},{13,15},{10,8},{11,9},{20,22},{21,... | collective-permute-start | bytes 4718600 | tf_op jit(solution)/shard_map/ppermute | solution.py:537
  281.5 41.2 %collective-permute-start.56 = (bf16[8,3,64,256]{3,2,1,0:T(8,128)(2,1)}, bf16[8,3,64,256]{3,2,1,0:T(8,128)(2,1)}, u32[]{:S(2)}, u32[]{:S(2)}) collective-permute-start(bf16[8,3,64,256]{3,2,1,0:T(8,128)(2,1)} %get-tuple-element.306), channel_id=1, source_target_pairs={{2,4},{3,5},{4,2},{5,3},{10,12},{11,13},{12,10},{13,11},{18,20},{1... | collective-permute-start | bytes 2359304 | tf_op jit(solution)/shard_map/ppermute | solution.py:531
  315.4 39.2 %collective-permute-start.58 = (bf16[8,3,64,512]{3,2,1,0:T(8,128)(2,1)S(1)}, bf16[8,3,64,512]{3,2,1,0:T(8,128)(2,1)S(1)}, u32[]{:S(2)}, u32[]{:S(2)}) collective-permute-start(bf16[8,3,64,512]{3,2,1,0:T(8,128)(2,1)S(1)} %get-tuple-element.312), channel_id=1, source_target_pairs={{4,6},{5,7},{2,0},{3,1},{12,14},{13,15},{10,8},{11,9},{20,22},{21,... | collective-permute-start | bytes 4718600 | tf_op jit(solution)/shard_map/ppermute | solution.py:537
  323.5 48.0 %collective-permute-start.60 = (bf16[8,3,64,256]{3,2,1,0:T(8,128)(2,1)S(1)}, bf16[8,3,64,256]{3,2,1,0:T(8,128)(2,1)S(1)}, u32[]{:S(2)}, u32[]{:S(2)}) collective-permute-start(bf16[8,3,64,256]{3,2,1,0:T(8,128)(2,1)S(1)} %get-tuple-element.315), channel_id=1, source_target_pairs={{4,6},{5,7},{2,0},{3,1},{12,14},{13,15},{10,8},{11,9},{20,22},{21,... | collective-permute-start | bytes 2359304 | tf_op jit(solution)/shard_map/ppermute | solution.py:537
  339.3 45.8 %collective-permute-start.57 = (bf16[8,3,64,256]{3,2,1,0:T(8,128)(2,1)S(1)}, bf16[8,3,64,256]{3,2,1,0:T(8,128)(2,1)S(1)}, u32[]{:S(2)}, u32[]{:S(2)}) collective-permute-start(bf16[8,3,64,256]{3,2,1,0:T(8,128)(2,1)S(1)} %get-tuple-element.311), channel_id=1, source_target_pairs={{4,6},{5,7},{2,0},{3,1},{12,14},{13,15},{10,8},{11,9},{20,22},{21,... | collective-permute-start | bytes 2359304 | tf_op jit(solution)/shard_map/ppermute | solution.py:537
  (59 other events, 655.0 us)
